TPU v7x, 32 devices: a whole 2x2x4 slice. The times are simulated.
32 devices in a mesh: dp: 8 (over y, x, core), blk: 4 (over z).
Axes of the slice: x: 2, y: 2, z: 4, core: 2. Of those that a mesh axis runs over, the one named last changes fastest.
Arguments:
- inputs: bfloat16 [8192, 1024], P(('dp', 'blk')), may hold values from -6 to 6
- positions: int32 [8192], P(('dp', 'blk')), may hold values from 0 to 1023, as said below
- w_query: bfloat16 [1024, 1024], P(('dp', 'blk')), may hold values from -0.21875 to 0.21875
- w_key: bfloat16 [1024, 1024], P(('dp', 'blk')), may hold values from -0.21875 to 0.21875
- w_value: bfloat16 [1024, 1024], P(('dp', 'blk')), may hold values from -0.1875 to 0.1875
- w_out: bfloat16 [1024, 1024], P(('dp', 'blk')), may hold values from -0.75 to 0.75
- w_up: bfloat16 [1024, 4096], P(('dp', 'blk')), may hold values from -0.1875 to 0.1875
- w_down: bfloat16 [4096, 1024], P(('dp', 'blk')), may hold values from -0.09375 to 0.09375
- up_bias: bfloat16 [4096], P(('dp', 'blk')), may hold values from -3 to 3
- down_bias: bfloat16 [1024], P(('dp', 'blk')), may hold values from -3 to 3
- ln1_gain: bfloat16 [1024], P(('dp', 'blk')), may hold values from 0.5 to 1.5
- ln1_bias: bfloat16 [1024], P(('dp', 'blk')), may hold values from -3 to 3
- ln2_gain: bfloat16 [1024], P(('dp', 'blk')), may hold values from 0.5 to 1.5
- ln2_bias: bfloat16 [1024], P(('dp', 'blk')), may hold values from -3 to 3
- cotangent: bfloat16 [8192, 1024], P(('dp', 'blk')), may hold values from -6 to 6
Outputs:
- output: bfloat16 [8192, 1024], P(('dp', 'blk'))
- input_grad: bfloat16 [8192, 1024], P(('dp', 'blk'))
- grad_query: float32 [1024, 1024], P(('dp', 'blk'))
- grad_key: float32 [1024, 1024], P(('dp', 'blk'))
- grad_value: float32 [1024, 1024], P(('dp', 'blk'))
- grad_out: float32 [1024, 1024], P(('dp', 'blk'))
- grad_up: float32 [1024, 4096], P(('dp', 'blk'))
- grad_down: float32 [4096, 1024], P(('dp', 'blk'))
- grad_up_bias: float32 [4096], P(('dp', 'blk'))
- grad_down_bias: float32 [1024], P(('dp', 'blk'))
- grad_ln1_gain: float32 [1024], P(('dp', 'blk'))
- grad_ln1_bias: float32 [1024], P(('dp', 'blk'))
- grad_ln2_gain: float32 [1024], P(('dp', 'blk'))
- grad_ln2_bias: float32 [1024], P(('dp', 'blk'))
Inputs may be any that keep to these rules, and one draw needn't show every extreme that they name: The rows of a group are its 1024 stream positions in order. A group holds either one sequence of 1024 tokens or two sequences of 512 tokens one after the other; positions count 0, 1, 2, ... from each sequence's start. 8 // 2 of the groups hold one sequence.
All inputs are finite; a program needn't handle non-finite values.
Results may differ from a plain program's by a relative error of at most 0.015.
Values may be sent and summed in bfloat16 or wider, within the bound.
A program may use at most 256 MiB of HBM per device.

v0:
```python
import math

import jax
import jax.numpy as jnp
from jax import lax
from jax.sharding import PartitionSpec as P

HEADS = 8


eps = 1e-05
masked_value = -1e30


def layer_norm(values, gain, offset):
    centre = jnp.mean(values, axis=-1, keepdims=True)
    centred = values - centre
    variance = jnp.mean(centred * centred, axis=-1, keepdims=True)
    return centred * lax.rsqrt(variance + eps) * gain + offset


def smooth_gate(values):
    return jax.nn.gelu(values, approximate=True)


def keep_same(carry):
    return carry


def local(
    inputs,
    positions,
    w_query,
    w_key,
    w_value,
    w_out,
    w_up,
    w_down,
    up_bias,
    down_bias,
    ln1_gain,
    ln1_bias,
    ln2_gain,
    ln2_bias,
    cotangent,
):
    attn_full = (
        lax.all_gather(w_query, ("dp", "blk"), axis=0, tiled=True),
        lax.all_gather(w_key, ("dp", "blk"), axis=0, tiled=True),
        lax.all_gather(w_value, ("dp", "blk"), axis=0, tiled=True),
        lax.all_gather(w_out, ("dp", "blk"), axis=0, tiled=True),
        lax.all_gather(ln1_gain, ("dp", "blk"), axis=0, tiled=True),
        lax.all_gather(ln1_bias, ("dp", "blk"), axis=0, tiled=True),
    )
    ffn_full = (
        lax.all_gather(w_up, ("dp", "blk"), axis=0, tiled=True),
        lax.all_gather(w_down, ("dp", "blk"), axis=0, tiled=True),
        lax.all_gather(up_bias, ("dp", "blk"), axis=0, tiled=True),
        lax.all_gather(down_bias, ("dp", "blk"), axis=0, tiled=True),
        lax.all_gather(ln2_gain, ("dp", "blk"), axis=0, tiled=True),
        lax.all_gather(ln2_bias, ("dp", "blk"), axis=0, tiled=True),
    )
    token_rows = inputs.astype(jnp.float32)
    local_rows, model_width = token_rows.shape
    head_count = HEADS
    head_size = model_width // head_count
    score_scale = 1.0 / math.sqrt(head_size)
    normed_first, first_pull = jax.vjp(
        layer_norm, token_rows, attn_full[4].astype(jnp.float32), attn_full[5].astype(jnp.float32)
    )
    normed_low = normed_first.astype(jnp.bfloat16)
    query_low = jnp.dot(normed_low, attn_full[0], preferred_element_type=jnp.float32).astype(
        jnp.bfloat16
    )
    key_low = jnp.dot(normed_low, attn_full[1], preferred_element_type=jnp.float32).astype(
        jnp.bfloat16
    )
    value_low = jnp.dot(normed_low, attn_full[2], preferred_element_type=jnp.float32).astype(
        jnp.bfloat16
    )
    keys_all, values_all = (
        lax.all_gather(key_low, "blk", axis=0, tiled=True),
        lax.all_gather(value_low, "blk", axis=0, tiled=True),
    )
    group_rows = keys_all.shape[0]
    key_rows = max(min(512, group_rows), local_rows)
    block_count = group_rows // key_rows
    first_row = lax.axis_index("blk") * local_rows
    query_index = first_row + jnp.arange(local_rows, dtype=jnp.int32)
    seq_start = query_index - positions
    earliest = jnp.min(seq_start)
    query_heads = query_low.reshape(local_rows, head_count, head_size)
    key_parts = []
    for which in range(block_count):
        begin = which * key_rows
        key_part = keys_all[begin : begin + key_rows].reshape(key_rows, head_count, head_size)
        value_part = values_all[begin : begin + key_rows].reshape(key_rows, head_count, head_size)
        key_index = begin + jnp.arange(key_rows, dtype=jnp.int32)
        allowed = (key_index[None, :] <= query_index[:, None]) & (
            key_index[None, :] >= seq_start[:, None]
        )
        needed = (begin <= first_row + local_rows - 1) & (begin + key_rows - 1 >= earliest)
        key_parts.append((key_part, value_part, allowed, needed))

    def scores_of(key_part, allowed):
        scores = (
            jnp.einsum("qhd,khd->hqk", query_heads, key_part, preferred_element_type=jnp.float32)
            * score_scale
        )
        return jnp.where(allowed[None], scores, masked_value)

    running_max = jnp.full((head_count, local_rows), masked_value, jnp.float32)
    running_sum = jnp.zeros((head_count, local_rows), jnp.float32)
    for key_part, value_part, allowed, needed in key_parts:

        def extend(carry):
            old_max, old_sum = carry
            scores = scores_of(key_part, allowed)
            new_max = jnp.maximum(old_max, jnp.max(scores, axis=-1))
            terms = jnp.where(allowed[None], jnp.exp(scores - new_max[..., None]), 0.0)
            return (new_max, old_sum * jnp.exp(old_max - new_max) + jnp.sum(terms, axis=-1))

        running_max, running_sum = lax.cond(needed, extend, keep_same, (running_max, running_sum))
    log_total = running_max + jnp.log(running_sum)

    def probs_of(key_part, allowed):
        scores = scores_of(key_part, allowed)
        return jnp.where(allowed[None], jnp.exp(scores - log_total[..., None]), 0.0)

    attended = jnp.zeros((local_rows, head_count, head_size), jnp.float32)
    for key_part, value_part, allowed, needed in key_parts:

        def gather_values(total):
            weights_low = probs_of(key_part, allowed).astype(jnp.bfloat16)
            return total + jnp.einsum(
                "hqk,khd->qhd", weights_low, value_part, preferred_element_type=jnp.float32
            )

        attended = lax.cond(needed, gather_values, keep_same, attended)
    mixed_low = attended.reshape(local_rows, model_width).astype(jnp.bfloat16)
    residual = token_rows + jnp.dot(mixed_low, attn_full[3], preferred_element_type=jnp.float32)
    normed_second, second_pull = jax.vjp(
        layer_norm, residual, ffn_full[4].astype(jnp.float32), ffn_full[5].astype(jnp.float32)
    )
    normed_two = normed_second.astype(jnp.bfloat16)
    preact = jnp.dot(normed_two, ffn_full[0], preferred_element_type=jnp.float32) + ffn_full[
        2
    ].astype(jnp.float32)
    gated, gate_pull = jax.vjp(smooth_gate, preact)
    hidden = gated.astype(jnp.bfloat16)
    output = (
        residual
        + jnp.dot(hidden, ffn_full[1], preferred_element_type=jnp.float32)
        + ffn_full[3].astype(jnp.float32)
    ).astype(jnp.bfloat16)
    up_back, down_back = (ffn_full[0], ffn_full[1])
    grad_final = cotangent.astype(jnp.float32)
    grad_down_w = jnp.einsum("tf,td->fd", hidden, cotangent, preferred_element_type=jnp.float32)
    grad_down_shift = jnp.sum(grad_final, axis=0)
    grad_hidden = jnp.einsum("td,fd->tf", cotangent, down_back, preferred_element_type=jnp.float32)
    grad_preact = gate_pull(grad_hidden)[0].astype(jnp.bfloat16)
    grad_up_shift = jnp.sum(grad_preact.astype(jnp.float32), axis=0)
    grad_up_w = jnp.einsum("td,tf->df", normed_two, grad_preact, preferred_element_type=jnp.float32)
    grad_normed_two = jnp.einsum(
        "tf,df->td", grad_preact, up_back, preferred_element_type=jnp.float32
    )
    grad_resid_two, grad_gain_two, grad_shift_two = second_pull(grad_normed_two)
    grad_residual = grad_final + grad_resid_two
    query_back, key_back, value_back, out_back = (
        attn_full[0],
        attn_full[1],
        attn_full[2],
        attn_full[3],
    )
    grad_branch = grad_residual.astype(jnp.bfloat16)
    grad_out_w = jnp.einsum("te,td->ed", mixed_low, grad_branch, preferred_element_type=jnp.float32)
    grad_mixed = jnp.einsum(
        "td,ed->te", grad_branch, out_back, preferred_element_type=jnp.float32
    ).astype(jnp.bfloat16)
    grad_heads = grad_mixed.reshape(local_rows, head_count, head_size)
    delta = jnp.zeros((head_count, local_rows), jnp.float32)
    for key_part, value_part, allowed, needed in key_parts:

        def add_delta(total):
            probs = probs_of(key_part, allowed)
            grad_probs = jnp.einsum(
                "qhd,khd->hqk", grad_heads, value_part, preferred_element_type=jnp.float32
            )
            return total + jnp.sum(probs * grad_probs, axis=-1)

        delta = lax.cond(needed, add_delta, keep_same, delta)
    grad_query_sum = jnp.zeros((local_rows, head_count, head_size), jnp.float32)
    kv_terms = []
    for key_part, value_part, allowed, needed in key_parts:

        def backward_part(total):
            probs = probs_of(key_part, allowed)
            grad_probs = jnp.einsum(
                "qhd,khd->hqk", grad_heads, value_part, preferred_element_type=jnp.float32
            )
            grad_scores = (probs * (grad_probs - delta[..., None]) * score_scale).astype(
                jnp.bfloat16
            )
            new_total = total + jnp.einsum(
                "hqk,khd->qhd", grad_scores, key_part, preferred_element_type=jnp.float32
            )
            grad_keys = jnp.einsum(
                "hqk,qhd->khd", grad_scores, query_heads, preferred_element_type=jnp.float32
            ).reshape(key_rows, model_width)
            grad_values = jnp.einsum(
                "hqk,qhd->khd",
                probs.astype(jnp.bfloat16),
                grad_heads,
                preferred_element_type=jnp.float32,
            ).reshape(key_rows, model_width)
            return (new_total, jnp.concatenate([grad_keys, grad_values], axis=1))

        def skip_part(total):
            return (total, jnp.zeros((key_rows, 2 * model_width), jnp.float32))

        grad_query_sum, kv_term = lax.cond(needed, backward_part, skip_part, grad_query_sum)
        kv_terms.append(kv_term)
    kv_shares = lax.psum_scatter(
        jnp.concatenate(kv_terms, axis=0).astype(jnp.bfloat16),
        "blk",
        scatter_dimension=0,
        tiled=True,
    ).astype(jnp.float32)
    grad_key_low = kv_shares[:, :model_width].astype(jnp.bfloat16)
    grad_value_low = kv_shares[:, model_width:].astype(jnp.bfloat16)
    grad_query_low = grad_query_sum.reshape(local_rows, model_width).astype(jnp.bfloat16)
    grad_query_w = jnp.einsum(
        "td,te->de", normed_low, grad_query_low, preferred_element_type=jnp.float32
    )
    grad_key_w = jnp.einsum(
        "td,te->de", normed_low, grad_key_low, preferred_element_type=jnp.float32
    )
    grad_value_w = jnp.einsum(
        "td,te->de", normed_low, grad_value_low, preferred_element_type=jnp.float32
    )
    grad_normed = (
        jnp.einsum("te,de->td", grad_query_low, query_back, preferred_element_type=jnp.float32)
        + jnp.einsum("te,de->td", grad_key_low, key_back, preferred_element_type=jnp.float32)
        + jnp.einsum("te,de->td", grad_value_low, value_back, preferred_element_type=jnp.float32)
    )
    grad_rows_one, grad_gain_one, grad_shift_one = first_pull(grad_normed)
    input_grad = (grad_residual + grad_rows_one).astype(jnp.bfloat16)
    shares = (
        lax.psum_scatter(grad_query_w, ("dp", "blk"), scatter_dimension=0, tiled=True),
        lax.psum_scatter(grad_key_w, ("dp", "blk"), scatter_dimension=0, tiled=True),
        lax.psum_scatter(grad_value_w, ("dp", "blk"), scatter_dimension=0, tiled=True),
        lax.psum_scatter(grad_out_w, ("dp", "blk"), scatter_dimension=0, tiled=True),
        lax.psum_scatter(grad_up_w, ("dp", "blk"), scatter_dimension=0, tiled=True),
        lax.psum_scatter(grad_down_w, ("dp", "blk"), scatter_dimension=0, tiled=True),
        lax.psum_scatter(grad_up_shift, ("dp", "blk"), scatter_dimension=0, tiled=True),
        lax.psum_scatter(grad_down_shift, ("dp", "blk"), scatter_dimension=0, tiled=True),
        lax.psum_scatter(grad_gain_one, ("dp", "blk"), scatter_dimension=0, tiled=True),
        lax.psum_scatter(grad_shift_one, ("dp", "blk"), scatter_dimension=0, tiled=True),
        lax.psum_scatter(grad_gain_two, ("dp", "blk"), scatter_dimension=0, tiled=True),
        lax.psum_scatter(grad_shift_two, ("dp", "blk"), scatter_dimension=0, tiled=True),
    )
    return (
        output,
        input_grad,
        shares[0],
        shares[1],
        shares[2],
        shares[3],
        shares[4],
        shares[5],
        shares[6],
        shares[7],
        shares[8],
        shares[9],
        shares[10],
        shares[11],
    )


def solution(mesh):
    in_specs = (
        P(("dp", "blk"), None),
        P(("dp", "blk")),
        P(("dp", "blk"), None),
        P(("dp", "blk"), None),
        P(("dp", "blk"), None),
        P(("dp", "blk"), None),
        P(("dp", "blk"), None),
        P(("dp", "blk"), None),
        P(("dp", "blk")),
        P(("dp", "blk")),
        P(("dp", "blk")),
        P(("dp", "blk")),
        P(("dp", "blk")),
        P(("dp", "blk")),
        P(("dp", "blk"), None),
    )
    out_specs = (
        P(("dp", "blk"), None),
        P(("dp", "blk"), None),
        P(("dp", "blk"), None),
        P(("dp", "blk"), None),
        P(("dp", "blk"), None),
        P(("dp", "blk"), None),
        P(("dp", "blk"), None),
        P(("dp", "blk"), None),
        P(("dp", "blk")),
        P(("dp", "blk")),
        P(("dp", "blk")),
        P(("dp", "blk")),
        P(("dp", "blk")),
        P(("dp", "blk")),
    )
    return jax.shard_map(local, mesh=mesh, in_specs=in_specs, out_specs=out_specs, check_vma=False)
```

profile of v0, /device:TPU:0, one launch (start us, length us, event | category | flops | bytes accessed | tf_op | source)
XLA Modules:
  0.0 1977.0 jit_solution(1268955338969438149)
XLA Ops:
  13.7 42.3 %all-reduce.12 = (bf16[1024]{0:T(1024)(128)(2,1)S(1)}, bf16[1024]{0:T(1024)(128)(2,1)S(1)}, bf16[1024]{0:T(1024)(128)(2,1)S(1)}, bf16[1024]{0:T(1024)(128)(2,1)S(1)}, bf16[1024]{0:T(1024)(128)(2,1)S(1)}) all-reduce(bf16[1024]{0:T(1024)(128)(2,1)S(1)} %dynamic-update-slice.1, ...), channel_id=1, replica_groups=mesh['dp'=8,'blk'=4] {'dp','blk'}, use_global_device_ids=true, to_apply=%add.1 | all-reduce | flops 5120 | bytes 20480
  56.0 1.2 convert_reduce_fusion.1
  57.2 1.3 fusion.86
  58.5 11.7 all-gather.12.cloned.1.call-done
  70.3 3.3 convolution_convert_fusion.2
  73.7 54.9 %all-gather.16.cloned.1.call-done = bf16[1024,1024]{1,0:T(8,128)(2,1)} async-done(((bf16[32,1024]{1,0:T(8,128)(2,1)}), bf16[1024,1024]{1,0:T(8,128)(2,1)}) %all-gather.16.cloned.1.call-update) | async-done | bytes 2097168 | tf_op jit(solution)/shard_map/all_gather | solution.py:50
  128.6 3.1 convolution_convert_fusion.1
  135.8 66.0 %all-gather = bf16[32,1,128]{2,1,0:T(2,128)(2,1)S(1)} all-gather(bf16[1,1,128]{2,1,0:T(2,128)(2,1)S(1)} %bitcast.115), channel_id=1, replica_groups=mesh['dp'=8,'blk'=4] {'dp','blk'}, dimensions={0}, use_global_device_ids=true | all-gather | bytes 8448 | tf_op jit(solution)/shard_map/all_gather | solution.py:58
  202.3 2.3 fusion.79
  204.7 28.9 %all-gather.14.cloned.1.call-done = bf16[1024,1024]{1,0:T(8,128)(2,1)} async-done(((bf16[256,1024]{1,0:T(8,128)(2,1)}), bf16[1024,1024]{1,0:T(8,128)(2,1)}) %all-gather.14.cloned.1.call-update) | async-done | bytes 2097168 | tf_op jit(solution)/shard_map/all_gather | solution.py:82
  233.7 1.7 slice_bitcast_fusion.2
  236.0 44.4 %all-gather.18.cloned.1.call-done = bf16[1024,1024]{1,0:T(8,128)(2,1)} async-done(((bf16[256,1024]{1,0:T(8,128)(2,1)}), bf16[1024,1024]{1,0:T(8,128)(2,1)}) %all-gather.18.cloned.1.call-update) | async-done | bytes 2097168 | tf_op jit(solution)/shard_map/all_gather | solution.py:83
  280.4 1.7 slice_bitcast_fusion
  282.1 1.3 copy.122
  283.4 1.3 copy.123
  284.7 3.9 conditional.8
  284.7 1.0 fusion
  286.3 2.2 select_reduce_fusion
  289.3 15.1 conditional.10
  300.1 4.2 convolution_bitcast_fusion
  304.3 2.2 copy.97
  306.5 31.9 %all-gather.20.cloned.1.call-done = bf16[1024,1024]{1,0:T(8,128)(2,1)} async-done(((bf16[32,1024]{1,0:T(8,128)(2,1)}), bf16[1024,1024]{1,0:T(8,128)(2,1)}) %all-gather.20.cloned.1.call-update) | async-done | bytes 2097168 | tf_op jit(solution)/shard_map/all_gather | solution.py:51
  338.4 2.6 fusion.114
  341.3 76.3 %all-gather.24.cloned.1.call-done = bf16[4096,1024]{1,0:T(8,128)(2,1)} async-done(((bf16[128,1024]{1,0:T(8,128)(2,1)}), bf16[4096,1024]{1,0:T(8,128)(2,1)}) %all-gather.24.cloned.1.call-update) | async-done | bytes 8388624 | tf_op jit(solution)/shard_map/all_gather | solution.py:57
  417.6 7.9 fusion.117
  425.5 71.1 %all-gather.22.cloned.1.call-done = bf16[1024,4096]{1,0:T(8,128)(2,1)} async-done(((bf16[32,4096]{1,0:T(8,128)(2,1)}), bf16[1024,4096]{1,0:T(8,128)(2,1)}) %all-gather.22.cloned.1.call-update) | async-done | bytes 8388624 | tf_op jit(solution)/shard_map/all_gather | solution.py:56
  496.6 11.6 convert_reduce_fusion
  508.1 1.3 copy-done.22
  509.4 2.6 multiply_reduce_fusion.2
  512.5 1.0 copy-done.3
  515.8 4.0 conditional.12
  515.8 2.1 fusion.26
  517.8 1.9 multiply_reduce_fusion
  520.0 18.2 conditional.14
  520.0 1.1 copy.106
  521.1 4.1 fusion.44
  525.2 2.1 copy.108
  527.4 4.8 multiply_convert_fusion
  532.2 1.8 convolution_bitcast_fusion.2
  534.7 1.5 fusion.36
  536.7 1.5 maximum_convert_fusion
  538.2 1.9 conditional.15
  538.2 1.5 broadcast.177
  540.1 4.8 pad_maximum_fusion
  544.9 1.4 copy.114
  546.3 2.8 fusion.104
  549.3 2.7 fusion.119
  552.0 87.5 %reduce-scatter.8.cloned.1.call-done = bf16[256,2048]{0,1:T(8,128)(2,1)} async-done(((bf16[1024,2048]{0,1:T(8,128)(2,1)}), bf16[256,2048]{0,1:T(8,128)(2,1)}) %reduce-scatter.8.cloned.1.call-update) | async-done | bytes 1048592 | tf_op jit(solution)/shard_map/reduce_scatter | solution.py:223
  639.5 4.0 fusion.93
  643.7 2.9 fusion.90
  646.8 9.8 fusion.100
  656.7 1.0 copy-done.7
  657.7 10.8 fusion.101
  668.5 2.4 fusion.118
  670.9 8.3 fusion.78
  680.8 1.0 fusion.109
  682.4 1.4 convert_reduce_fusion.2
  683.7 42.1 %all-reduce.11 = (f32[4096]{0:T(1024)S(1)}, f32[1024]{0:T(1024)S(1)}, f32[1024]{0:T(1024)S(1)}, f32[1024]{0:T(1024)S(1)}, f32[1024]{0:T(1024)S(1)}, /*index=5*/f32[1024]{0:T(1024)S(1)}) all-reduce(f32[4096]{0:T(1024)S(1)} %get-tuple-element.372, ...), channel_id=9, replica_groups=mesh['dp'=8,'blk'=4] {'dp','blk'}, use_global_device_ids=true, to_apply=%region_39.40.clone | all-reduce | flops 9216 | bytes 73728
  729.4 61.5 %reduce-scatter.10.cloned.1.call-done = f32[32,1024]{1,0:T(8,128)} async-done(((f32[1024,1024]{1,0:T(8,128)}), f32[32,1024]{1,0:T(8,128)}) %reduce-scatter.10.cloned.1.call-update) | async-done | bytes 131088 | tf_op jit(solution)/shard_map/reduce_scatter | solution.py:249
  790.9 149.3 %reduce-scatter.16.cloned.1.call-done = f32[32,1024]{1,0:T(8,128)} async-done(((f32[1024,1024]{1,0:T(8,128)}), f32[32,1024]{1,0:T(8,128)}) %reduce-scatter.16.cloned.1.call-update) | async-done | bytes 131088 | tf_op jit(solution)/shard_map/reduce_scatter | solution.py:252
  940.2 149.4 %reduce-scatter.12.cloned.1.call-done = f32[32,1024]{1,0:T(8,128)} async-done(((f32[1024,1024]{1,0:T(8,128)}), f32[32,1024]{1,0:T(8,128)}) %reduce-scatter.12.cloned.1.call-update) | async-done | bytes 131088 | tf_op jit(solution)/shard_map/reduce_scatter | solution.py:250
  1089.6 149.6 %reduce-scatter.14.cloned.1.call-done = f32[32,1024]{1,0:T(8,128)} async-done(((f32[1024,1024]{1,0:T(8,128)}), f32[32,1024]{1,0:T(8,128)}) %reduce-scatter.14.cloned.1.call-update) | async-done | bytes 131088 | tf_op jit(solution)/shard_map/reduce_scatter | solution.py:251
  1239.2 366.0 %reduce-scatter.18.cloned.1.call-done = f32[32,4096]{1,0:T(8,128)} async-done(((f32[1024,4096]{1,0:T(8,128)}), f32[32,4096]{1,0:T(8,128)}) %reduce-scatter.18.cloned.1.call-update) | async-done | bytes 524304 | tf_op jit(solution)/shard_map/reduce_scatter | solution.py:253
  1605.2 365.0 %reduce-scatter.20.cloned.1.call-done = f32[128,1024]{1,0:T(8,128)} async-done(((f32[4096,1024]{1,0:T(8,128)}), f32[128,1024]{1,0:T(8,128)}) %reduce-scatter.20.cloned.1.call-update) | async-done | bytes 524304 | tf_op jit(solution)/shard_map/reduce_scatter | solution.py:254
  (126 shorter events, 22.1 us)
Async XLA Ops:
  7.2 121.4 %copy-start = (bf16[256,1024]{1,0:T(8,128)(2,1)S(1)}, bf16[256,1024]{1,0:T(8,128)(2,1)}, u32[]{:S(2)}) copy-start(bf16[256,1024]{1,0:T(8,128)(2,1)} %param.31) | copy-start | bytes 1572868
  7.2 63.1 %all-gather.12.cloned.1.call-start = ((), (), s32[]{:S(2)}) async-start(), calls=%async_computation.8 | async-start | bytes 2162688 | tf_op jit(solution)/shard_map/all_gather | solution.py:49
  7.9 120.7 %all-gather.16.cloned.1.call-start = ((), (), s32[]{:S(2)}) async-start(), calls=%async_computation.10 | async-start | bytes 2162688 | tf_op jit(solution)/shard_map/all_gather | solution.py:50
  8.7 193.6 %all-gather.10.cloned.1.call-start = ((), (), s32[]{:S(2)}) async-start(), calls=%async_computation.7 | async-start | bytes 2162688 | tf_op jit(solution)/shard_map/all_gather | solution.py:48
  9.4 224.3 %all-gather.14.cloned.1.call-start = ((), (), s32[]{:S(2)}) async-start(), calls=%async_computation.9 | async-start | bytes 2621440 | tf_op jit(solution)/shard_map/all_gather | solution.py:82
  58.5 75.4 %copy-start.27 = (s32[256]{0:T(256)S(1)}, s32[256]{0:T(256)}, u32[]{:S(2)}) copy-start(s32[256]{0:T(256)} %param.32) | copy-start | bytes 3076
  73.6 62.2 %copy-start.28 = (bf16[128]{0:T(256)(128)(2,1)S(1)}, bf16[128]{0:T(256)(128)(2,1)}, u32[]{:S(2)}) copy-start(bf16[128]{0:T(256)(128)(2,1)} %param.39) | copy-start | bytes 772
  73.6 206.8 %all-gather.18.cloned.1.call-start = ((), (), s32[]{:S(2)}) async-start(), calls=%async_computation.11 | async-start | bytes 2621440 | tf_op jit(solution)/shard_map/all_gather | solution.py:83
  131.8 206.7 %all-gather.20.cloned.1.call-start = ((), (), s32[]{:S(2)}) async-start(), calls=%async_computation.12 | async-start | bytes 2162688 | tf_op jit(solution)/shard_map/all_gather | solution.py:51
  132.3 285.3 %all-gather.24.cloned.1.call-start = ((), (), s32[]{:S(2)}) async-start(), calls=%async_computation.14 | async-start | bytes 8650752 | tf_op jit(solution)/shard_map/all_gather | solution.py:57
  133.1 363.5 %all-gather.22.cloned.1.call-start = ((), (), s32[]{:S(2)}) async-start(), calls=%async_computation.13 | async-start | bytes 8650752 | tf_op jit(solution)/shard_map/all_gather | solution.py:56
  133.8 505.7 %reduce-scatter.8.cloned.1.call-start = ((), (), s32[]{:S(2)}) async-start(), calls=%async_computation.15 | async-start | bytes 5242880 | tf_op jit(solution)/shard_map/reduce_scatter | solution.py:223
  235.7 53.6 %copy-start.1 = (bf16[64,8,8,128]{3,2,1,0:T(8,128)(2,1)}, bf16[64,8,8,128]{3,2,1,0:T(8,128)(2,1)S(1)}, u32[]{:S(2)}) copy-start(bf16[64,8,8,128]{3,2,1,0:T(8,128)(2,1)S(1)} %copy.120) | copy-start | bytes 3145732
  496.6 12.9 copy-start.29
  508.1 1.3 copy-start.22
  509.4 4.1 copy-start.6
  512.1 2.0 copy-start.17
  512.5 1.0 copy-start.3
  514.1 0.8 copy-start.20
  515.8 2.1 copy-start.8
  515.8 2.1 copy-start.24
  527.4 4.8 copy-start.2
  527.4 6.6 copy-start.26
  532.2 2.6 copy-start.16
  534.7 1.5 copy-start.12
  544.8 246.1 %reduce-scatter.10.cloned.1.call-start = ((), (), s32[]{:S(2)}) async-start(), calls=%async_computation.16 | async-start | bytes 4325376 | tf_op jit(solution)/shard_map/reduce_scatter | solution.py:249
  546.3 2.9 copy-start.5
  546.3 2.9 copy-start.21
  549.2 391.0 %reduce-scatter.16.cloned.1.call-start = ((), (), s32[]{:S(2)}) async-start(), calls=%async_computation.19 | async-start | bytes 4325376 | tf_op jit(solution)/shard_map/reduce_scatter | solution.py:252
  552.0 537.6 %reduce-scatter.12.cloned.1.call-start = ((), (), s32[]{:S(2)}) async-start(), calls=%async_computation.17 | async-start | bytes 4325376 | tf_op jit(solution)/shard_map/reduce_scatter | solution.py:250
  639.5 4.1 copy-start.13
  643.6 595.5 %reduce-scatter.14.cloned.1.call-start = ((), (), s32[]{:S(2)}) async-start(), calls=%async_computation.18 | async-start | bytes 4325376 | tf_op jit(solution)/shard_map/reduce_scatter | solution.py:251
  646.6 958.6 %reduce-scatter.18.cloned.1.call-start = ((), (), s32[]{:S(2)}) async-start(), calls=%async_computation.20 | async-start | bytes 17301504 | tf_op jit(solution)/shard_map/reduce_scatter | solution.py:253
  656.6 1.0 copy-start.7
  656.7 1313.6 %reduce-scatter.20.cloned.1.call-start = ((), (), s32[]{:S(2)}) async-start(), calls=%async_computation.21 | async-start | bytes 17301504 | tf_op jit(solution)/shard_map/reduce_scatter | solution.py:254
  670.8 8.4 copy-start.14
  670.9 8.4 copy-start.18
  679.2 1.6 copy-start.19
  680.8 1.6 copy-start.4
Sparse Core Ops, SparseCore 0:
  11.0 59.2 all-gather.11
  73.2 55.3 all-gather.15
  131.5 55.3 all-gather.9
  188.9 44.7 all-gather.13
  235.7 44.6 all-gather.17
  283.2 55.1 all-gather.19
  341.3 76.2 all-gather.23
  420.5 75.9 all-gather.21
  545.0 94.5 reduce-scatter.7
  642.3 148.5 reduce-scatter.9
  793.8 146.2 reduce-scatter.15
  943.0 146.5 reduce-scatter.11
  1092.5 146.6 reduce-scatter.13
  1242.0 363.1 reduce-scatter.17
  1608.0 362.1 reduce-scatter.19
where the time goes:
time: 1990 us; the launch traced here: 1980 us
  waiting for transfers between devices  1650 us (83%)
  blocking collectives  150 us (8%)
  matrix products  101 us (5%)
  local copies, waits for them, and re-layouts  28.9 us (1%)
    reduce_scatter x1, waiting for transfers between devices, local(): lax.psum_scatter(grad_up_w, ('dp', 'blk'), scatter_dimension=0, tiled=True)  366 us
    reduce_scatter x1, waiting for transfers between devices, local(): lax.psum_scatter(grad_down_w, ('dp', 'blk'), scatter_dimension=0, tiled=T...  365 us
    reduce_scatter x1, waiting for transfers between devices, local(): lax.psum_scatter(grad_value_w, ('dp', 'blk'), scatter_dimension=0, tiled=...  150 us
    reduce_scatter x1, waiting for transfers between devices, local(): lax.psum_scatter(grad_key_w, ('dp', 'blk'), scatter_dimension=0, tiled=True)  149 us
    reduce_scatter x1, waiting for transfers between devices, local(): lax.psum_scatter(grad_out_w, ('dp', 'blk'), scatter_dimension=0, tiled=True)  149 us
    reduce_scatter x1, waiting for transfers between devices, local(): lax.psum_scatter(jnp.concatenate(kv_terms, axis=0).astype(jnp.bfloat16),...  87.5 us
    unnamed x2, blocking collectives  84.5 us
    all_gather x1, waiting for transfers between devices, local(): lax.all_gather(w_down, ('dp', 'blk'), axis=0, tiled=True)  76.3 us
  transfers between devices with their start and end apart: 15, of which 14 were waited for; matrix products, arithmetic and copies ran while one was open for 5% of the time, Pallas kernels for 0%

commit v1 on v0

--- a/solution.py
+++ b/solution.py
@@ -1,15 +1,1114 @@
+import functools
 import math
+import types
 
 import jax
 import jax.numpy as jnp
 from jax import lax
+from jax.experimental import pallas as pl
+from jax.experimental.pallas import tpu as pltpu
 from jax.sharding import PartitionSpec as P
 
+MESH = pl.DeviceIdType.MESH
+F32 = jnp.float32
+BF16 = jnp.bfloat16
 HEADS = 8
-
-
+VMEM_BYTES = 60 * 2**20
+RANKS = 4
 eps = 1e-05
 masked_value = -1e30
+GELU_K = math.sqrt(2.0 / math.pi)
+GELU_C = 0.044715
+
+
+def dot_nn(a, b):
+    return lax.dot_general(a, b, (((1,), (0,)), ((), ())), preferred_element_type=F32)
+
+
+def dot_nt(a, b):
+    return lax.dot_general(a, b, (((1,), (1,)), ((), ())), preferred_element_type=F32)
+
+
+def dot_tn(a, b):
+    return lax.dot_general(a, b, (((0,), (0,)), ((), ())), preferred_element_type=F32)
+
+
+def norm_parts(v):
+    centre = jnp.mean(v, axis=-1, keepdims=True)
+    centred = v - centre
+    variance = jnp.mean(centred * centred, axis=-1, keepdims=True)
+    rstd = lax.rsqrt(variance + eps)
+    return centred * rstd, rstd
+
+
+def norm_back(g, gain, xhat, rstd):
+    e = g * gain
+    return rstd * (
+        e
+        - jnp.mean(e, axis=-1, keepdims=True)
+        - xhat * jnp.mean(e * xhat, axis=-1, keepdims=True)
+    )
+
+
+def hidden_at(k, tt):
+    return ((k // 2) * 2 + tt % 2) * 4 + (k % 2) * 2 + tt // 2
+
+
+IN_NAMES = ("x_in", "dz_in", "pos", "wq", "wk", "wv", "wo", "wup", "wdn", "db", "g1", "b1", "g2", "b2", "ub")
+OUT_NAMES = ("out", "ig", "peq", "peu", "go", "gdn", "gvec")
+
+
+def scratch_of(rows, width, hid, rw, fw):
+    half = rows // 2
+    hd = width // HEADS
+    cols = 3 * 2 * hd
+    dma = pltpu.SemaphoreType.DMA
+    V = pltpu.VMEM
+    names = dict(
+        X=V((4, 2, half, width), BF16),
+        DZ=V((4, 2, half, width), BF16),
+        ST=V((4, 2, 16, 128), BF16),
+        WA=V((4, 2, 2, 2 * rw, cols), BF16),
+        WOP=V((8, rw, width), BF16),
+        WO=V((2, 2, 2, rw, width), BF16),
+        VEC=V((8, 16, width), BF16),
+        WU=V((4, 2, 2, 2 * rw, hid), BF16),
+        WD=V((8, fw, width), BF16),
+        PV=V((4, 16, width), BF16),
+        VF=V((8, width), F32),
+        SV=V((8, rw), F32),
+        VT=V((16, width), F32),
+        vec=V((16, width), BF16),
+        st_in=V((16, 128), BF16),
+        TU=V((256, 4 * rows), BF16),
+        N1=V((4 * rows, width), BF16),
+        QKV=V((4 * rows, cols), BF16),
+        P0=V((2, rows, rows), BF16),
+        P1=V((2, rows, 2 * rows), BF16),
+        P2=V((2, rows, 3 * rows), BF16),
+        P3=V((2, rows, 4 * rows), BF16),
+        MIX=V((4 * rows, 2 * hd), BF16),
+        DMIX=V((rows, 2 * hd), BF16),
+        PR0=V((4, 2, half, width), BF16),
+        PR1=V((4, 2, half, width), BF16),
+        RBa=V((4, half, width), BF16),
+        RBb=V((4, half, width), BF16),
+        RBc=V((4, half, width), BF16),
+        RXa=V((4, half, width), BF16),
+        RXb=V((2, half, width), BF16),
+        RXc=V((4, half, width), BF16),
+        RXd=V((2, half, width), BF16),
+        RES=V((4, half, width), F32),
+        KEEP=V((2, half, width), F32),
+        N2=V((4, 2, half, width), BF16),
+        HID=V((4 * rows, hid), BF16),
+        DP=V((4 * rows, hid), BF16),
+        DB=V((4, 2, half, width), BF16),
+        ACC=V((4 * rows, 4 * hd), F32),
+        TT=V((width // 2, 4 * rows), BF16),
+        YSF=V((2, 4, fw, width), BF16),
+        R1F=V((2, 4, fw, width), BF16),
+        R2F=V((2, 2, fw, width), BF16),
+        R3F=V((2, fw, width), BF16),
+        YSQ=V((2, 4, 2 * rw, cols), BF16),
+        R1Q=V((2, 4, 2 * rw, cols), BF16),
+        R2Q=V((2, 2, 2 * rw, cols), BF16),
+        R3Q=V((2, 2 * rw, cols), BF16),
+        GOB=V((2, 2, 2, rw, width), BF16),
+        GOR=V((2, 2, rw, width), BF16),
+        GOS=V((8, rw, width), BF16),
+        GOT=V((8, rw, width), BF16),
+        OD=V((fw, width), F32),
+        OO=V((rw, width), F32),
+        OUTB=V((2, half, width), BF16),
+        IGB=V((2, half, width), BF16),
+        VSUM=V((8, width), F32),
+        VMID=V((8, width), F32),
+        VR1=V((4, 8, width), F32),
+        VR2=V((8, 8, width), F32),
+        sp_s=dma((3, 8)),
+        sp_r=dma((3, 4, 2)),
+        loc=dma((4,)),
+        load=dma((7,)),
+        pre_s=dma((3, 3)),
+        pre_r=dma((3, 4)),
+        ag_s=dma((6, 7)),
+        ag_r=dma((6, 8)),
+        sw_s=dma((4,)),
+        sw_r=dma((4,)),
+        sw_s2=dma((4,)),
+        sw_r2=dma((4,)),
+        FIN=V((2, 2 * rw, cols), BF16),
+        FIU=V((fw, hid), BF16),
+        sib_s=dma((4, 4)),
+        sib_r=dma((4, 4)),
+        xs=dma((4, 4)),
+        xr=dma((4, 4)),
+        n2_s=dma((4,)),
+        n2_r=dma((4,)),
+        db_s=dma((4,)),
+        db_r=dma((4,)),
+        r1_s=dma((4, 4)),
+        r1_r=dma((4, 4)),
+        up_s=dma((4, 4)),
+        up_r=dma((4, 4)),
+        r2_s=dma((4, 2)),
+        r2_r=dma((4, 2)),
+        r3_s=dma((4,)),
+        r3_r=dma((4,)),
+        go_s=dma((8,)),
+        go_r=dma((8,)),
+        pe_s=dma((2, 4)),
+        pe_r=dma((2, 4)),
+        v1_s=dma((3,)),
+        v1_r=dma((4,)),
+        v2_s=dma((7,)),
+        v2_r=dma((8,)),
+        ret_s=dma((2, 2)),
+        ret_r=dma((2, 2)),
+    )
+    return names
+
+
+def fused(names, *all_refs):
+    m = types.SimpleNamespace(**dict(zip(names, all_refs)))
+    half, width = m.X.shape[2:]
+    rows = 2 * half
+    hid = m.HID.shape[1]
+    rw = m.WOP.shape[1]
+    fw = m.WD.shape[1]
+    hd = width // HEADS
+    two = 2 * hd
+    scale = 1.0 / math.sqrt(hd)
+
+    dp = lax.axis_index("dp")
+    z = lax.axis_index("blk")
+    yx = lax.div(dp, 2)
+    y, x, c = lax.div(dp, 4), lax.rem(yx, 2), lax.rem(dp, 2)
+    q, p = lax.div(z, 2), lax.rem(z, 2)
+    t = p * 2 + c
+    me = yx * 2 + q
+
+    def dev(yy, xx, cc, zz):
+        return ((yy * 2 + xx) * 2 + cc, zz)
+
+    def mate(tt):
+        return dev(y, x, lax.rem(tt, 2), q * 2 + lax.div(tt, 2))
+
+    def peer(yy, xx, qq):
+        return dev(yy, xx, c, qq * 2 + p)
+
+    def at8(yy, xx, qq):
+        return yy * 4 + xx * 2 + qq
+
+    sib = dev(y, x, 1 - c, z)
+    nbr = dev(y, x, c, q * 2 + 1 - p)
+    over = {"q": peer(y, x, 1 - q), "x": peer(y, 1 - x, q), "y": peer(1 - y, x, q)}
+
+    mine = (p, p + 2)
+    theirs = (1 - p, 3 - p)
+
+    sent = []
+
+    def remote(src, dst, ssem, rsem, device):
+        return pltpu.make_async_remote_copy(
+            src_ref=src,
+            dst_ref=dst,
+            send_sem=ssem,
+            recv_sem=rsem,
+            device_id=device,
+            device_id_type=MESH,
+        )
+
+    def push(src, dst, ssem, rsem, device, keep=True):
+        copy = remote(src, dst, ssem, rsem, device)
+        copy.start()
+        if keep:
+            sent.append(copy)
+        return copy
+
+    homes = []
+
+    def push_if(cond, src, dst, ssem, rsem, device):
+        copy = remote(src, dst, ssem, rsem, device)
+
+        @pl.when(cond)
+        def _():
+            copy.start()
+
+        homes.append((jnp.logical_not(cond), copy))
+
+    def arrived(dst, rsem):
+        pltpu.make_async_copy(dst, dst, rsem).wait()
+
+    loads = [pltpu.make_async_copy(ref, m.PR1.at[k, 0, pl.ds(0, rw)], m.load.at[k]) for k, ref in enumerate((m.wq, m.wk, m.wv))]
+    loads += [
+        pltpu.make_async_copy(m.wup.at[:, pl.ds(k * width, width)], m.PR1.at[k, 1, pl.ds(0, rw)], m.load.at[3 + k])
+        for k in range(4)
+    ]
+    for copy in loads:
+        copy.start()
+    m.st_in[...] = jnp.broadcast_to((z * rows - m.pos[0:1, 0:1]).astype(F32), (16, 128)).astype(BF16)
+    for k, ref in enumerate((m.db, m.g1, m.b1, m.g2, m.b2)):
+        m.SV[k : k + 1] = ref[...].astype(F32)
+    m.SV[5:8] = jnp.zeros((3, rw), F32)
+    spot = lax.broadcasted_iota(jnp.int32, (rw, width), 1) - (dp * 4 + z) * rw
+    hot = jnp.where(spot == lax.broadcasted_iota(jnp.int32, (rw, width), 0), 1.0, 0.0).astype(BF16)
+    m.VT[0:8] = dot_nn(m.SV[...].astype(BF16), hot)
+    m.VT[8:16] = jnp.zeros((8, width), F32)
+    m.VT[5:6, pl.ds(pl.multiple_of(me * fw, 128), fw)] = m.ub[...].astype(F32)
+    m.vec[...] = m.VT[...].astype(BF16)
+
+    barrier = pltpu.get_barrier_semaphore()
+    flips = [(a, b, d) for a in range(2) for b in range(2) for d in range(2)]
+
+    def flipped(a, b, d):
+        return ((1 - y if a else y), (1 - x if b else x), (1 - q if d else q))
+
+    others = [dev(y, x, lax.rem(c + a, 2), lax.rem(z + b, 4)) for a in range(2) for b in range(4) if a or b] + [
+        peer(*flipped(*f)) for f in flips if f[0] or f[1]
+    ]
+    for device in others:
+        pl.semaphore_signal(barrier, inc=1, device_id=device, device_id_type=MESH)
+    pl.semaphore_wait(barrier, len(others))
+
+    def half_rows(ref):
+        return lambda k: ref.at[pl.ds(k * half, half)]
+
+    streams = (
+        (half_rows(m.x_in), m.X),
+        (lambda k: m.st_in, m.ST),
+        (half_rows(m.dz_in), m.DZ),
+    )
+    to_z = 2 * c + p
+
+    def spread_home(k):
+        src, buf = streams[k]
+        for cc in range(2):
+            own = (q == c) & (c == cc)
+            dst = buf.at[z, cc]
+            rsem = m.sp_r.at[k, z, cc]
+
+            @pl.when(own)
+            def _():
+                pltpu.make_async_copy(src(cc), dst, rsem).start()
+
+            copy = remote(src(cc), dst, m.sp_s.at[k, cc], rsem, dev(y, x, cc, to_z))
+
+            @pl.when(jnp.logical_not(own))
+            def _():
+                copy.start()
+
+            homes.append((own, copy))
+
+    def spread_own(k):
+        _, buf = streams[k]
+        for kk in range(2):
+            i = mine[kk]
+            arrived(buf.at[i, c], m.sp_r.at[k, i, c])
+            push(buf.at[i, c], buf.at[i, c], m.sp_s.at[k, 2 + 2 * kk], m.sp_r.at[k, i, c], nbr)
+            push(buf.at[i, c], buf.at[i, c], m.sp_s.at[k, 3 + 2 * kk], m.sp_r.at[k, i, c], sib)
+
+    def spread_nbr(k):
+        _, buf = streams[k]
+        for kk in range(2):
+            j = theirs[kk]
+            arrived(buf.at[j, c], m.sp_r.at[k, j, c])
+            push(buf.at[j, c], buf.at[j, c], m.sp_s.at[k, 6 + kk], m.sp_r.at[k, j, c], sib)
+
+    def spread_end(k):
+        _, buf = streams[k]
+        for i in mine + theirs:
+            arrived(buf.at[i, 1 - c], m.sp_r.at[k, i, 1 - c])
+
+    spread_home(0)
+    spread_home(1)
+
+    for copy in loads:
+        copy.wait()
+    for tt in range(4):
+        at = 0
+        for k in range(3):
+            for j in range(2):
+                m.PR0[tt, 1, 0:rw, at : at + hd] = m.PR1[k, 0, 0:rw, (j * 4 + tt) * hd : (j * 4 + tt + 1) * hd]
+                at += hd
+        for k in range(8):
+            row, at = divmod(hidden_at(k, tt) * fw, width)
+            m.PR0[tt, 0, 0:rw, k * fw : (k + 1) * fw] = m.PR1[row, 1, 0:rw, at : at + fw]
+    cols = 3 * two
+
+    def pre_src(n, tt):
+        if n == 0:
+            return m.PR0.at[tt, 1, pl.ds(0, rw), pl.ds(0, cols)]
+        if n == 1:
+            return m.vec
+        return m.PR0.at[tt, 0, pl.ds(0, rw), pl.ds(0, hid)]
+
+    def rank_rows(cc, pp):
+        return (yx, cc, q, pl.ds(pl.multiple_of(pp * rw, rw), rw))
+
+    def pre_dst(n, tt):
+        if n == 1:
+            return m.PV.at[tt]
+        return (m.WA if n == 0 else m.WU).at[rank_rows(lax.rem(tt, 2), lax.div(tt, 2))]
+
+    pre_sent = []
+    for n in (1, 0, 2):
+        for d in (1, 2, 3):
+            tt = lax.rem(t + d, 4)
+            pre_sent.append(
+                push(pre_src(n, tt), pre_dst(n, t), m.pre_s.at[n, d - 1], m.pre_r.at[n, t], mate(tt), keep=False)
+            )
+    local_o = pltpu.make_async_copy(m.wo, m.WOP.at[me], m.loc.at[0])
+    local_o.start()
+    local_d = pltpu.make_async_copy(m.wdn, m.WD.at[me], m.loc.at[1])
+    local_d.start()
+    m.WA[rank_rows(c, p)] = m.PR0[t, 1, 0:rw, 0:cols]
+    m.WU[rank_rows(c, p)] = m.PR0[t, 0, 0:rw, 0:hid]
+    m.PV[t] = m.vec[...]
+
+    def pre_wait(n):
+        for d in (1, 2, 3):
+            tt = lax.rem(t + d, 4)
+            arrived(pre_dst(n, tt), m.pre_r.at[n, tt])
+
+    def piece(n, yy, xx, qq):
+        if n < 2:
+            return m.WA.at[yy * 2 + xx, n, qq]
+        if n == 4:
+            return m.WU.at[yy * 2 + xx, :, qq]
+        return {2: m.VEC, 3: m.WOP, 5: m.WD}[n].at[at8(yy, xx, qq)]
+
+    def order(n):
+        return "xy" if n in (0, 2, 4) else "yx"
+
+    def beyond(first, qq):
+        return (y, 1 - x, qq) if first == "x" else (1 - y, x, qq)
+
+    def gather_send(n, spot, k, to):
+        ref = piece(n, *spot)
+        push(ref, ref, m.ag_s.at[n, k], m.ag_r.at[n, at8(*spot)], over[to])
+
+    def gather_own(group):
+        for k in range(3):
+            for n in group:
+                gather_send(n, (y, x, q), k, ("q" + order(n))[k])
+
+    def gather_pass(group, k):
+        for n in group:
+            first, second = order(n)
+            spot = (y, x, 1 - q) if k == 0 else beyond(first, q if k == 1 else 1 - q)
+            arrived(piece(n, *spot), m.ag_r.at[n, at8(*spot)])
+            if k == 0:
+                gather_send(n, spot, 3, first)
+                gather_send(n, spot, 4, second)
+            else:
+                gather_send(n, spot, 4 + k, second)
+
+    def gather_end(group):
+        for n in group:
+            second = order(n)[1]
+            for a in range(2):
+                for qq in range(2):
+                    spot = (1 - y, a, qq) if second == "y" else (a, 1 - x, qq)
+                    arrived(piece(n, *spot), m.ag_r.at[n, at8(*spot)])
+
+    VECS, ATT, WOUT, FFN = (2,), (0, 1), (3,), (4, 5)
+
+    def norm_one(i, h):
+        xhat, _ = norm_parts(m.X[i, h].astype(F32))
+        at = pl.ds(pl.multiple_of(i * rows + h * half, half), half)
+        m.N1[at, :] = (xhat * m.VF[1:2] + m.VF[2:3]).astype(BF16)
+
+    pre_wait(1)
+    total = sum((m.PV[a].astype(F32) for a in range(1, 4)), m.PV[0].astype(F32))
+    line = lax.broadcasted_iota(jnp.int32, (16, width), 0)
+    own_vec = jnp.where(line == 5, m.vec[...].astype(F32), total)
+    m.VEC[me] = own_vec.astype(BF16)
+    gather_own(VECS)
+    pre_wait(0)
+    gather_own(ATT)
+    local_o.wait()
+    local_d.wait()
+    pre_wait(2)
+    for copy in pre_sent:
+        copy.wait_send()
+    gather_pass(VECS, 0)
+    gather_pass(VECS, 1)
+    gather_pass(VECS, 2)
+    spread_own(0)
+    spread_own(1)
+    gather_pass(ATT, 0)
+    gather_own(WOUT)
+    gather_own(FFN)
+    gather_end(VECS)
+    every = m.VEC[0].astype(F32)
+    for a in range(1, 8):
+        every = every + m.VEC[a].astype(F32)
+    m.VF[...] = every[0:8]
+    for i in mine:
+        norm_one(i, c)
+    gather_pass(ATT, 1)
+    spread_nbr(0)
+    spread_nbr(1)
+    gather_pass(ATT, 2)
+    spread_home(2)
+    for i in theirs:
+        norm_one(i, c)
+    spread_end(0)
+    spread_end(1)
+    for i in mine + theirs:
+        norm_one(i, 1 - c)
+    for k in range(3):
+        gather_pass(WOUT, k)
+    gather_end(ATT)
+
+    def swap_out():
+        gather_end(WOUT)
+        for yy in range(2):
+            for qq in range(2):
+                k = yy * 2 + qq
+                push(
+                    m.WOP.at[at8(yy, 1 - p, qq)], m.WO.at[yy, qq, p], m.sw_s.at[k], m.sw_r.at[k], nbr
+                )
+                m.WO[yy, qq, p] = m.WOP[at8(yy, p, qq)]
+
+    def swap_end():
+        for yy in range(2):
+            for qq in range(2):
+                arrived(m.WO.at[yy, qq, 1 - p], m.sw_r.at[yy * 2 + qq])
+
+    def row_tile(i):
+        return pl.ds(pl.multiple_of(i * rows, rows), rows)
+
+    def col_tile(n, size=256):
+        return pl.ds(pl.multiple_of(n * size, size), size)
+
+    @pl.loop(0, 3)
+    def _(n):
+        w = m.WA[:, :, :, :, col_tile(n)].reshape(width, 256)
+
+        @pl.loop(0, 4)
+        def _(i):
+            m.QKV[row_tile(i), col_tile(n)] = dot_nn(m.N1[row_tile(i), :], w).astype(BF16)
+
+    EX = (
+        (m.PR0, m.RBa, m.RXa),
+        (m.PR1, m.RBb, m.RXb),
+        (m.PR0, m.RBa, m.RXc),
+        (m.PR1, m.RBc, m.RXd),
+    )
+    ex_open = {}
+    ex_far = {1: [], 3: []}
+
+    def ex_put(e, i, cols_at, value):
+        pair = EX[e][0]
+        low = value.astype(BF16)
+        pair[i, 0, :, cols_at] = low[0:half]
+        pair[i, 1, :, cols_at] = low[half:rows]
+
+    def ex_send(e, i):
+        pair, rb, _ = EX[e]
+        ex_open[e, i] = [push(pair.at[i, 1 - c], rb.at[i], m.sib_s.at[e, i], m.sib_r.at[e, i], sib, keep=False)]
+
+    def ex_mid(e, i):
+        pair, rb, rx = EX[e]
+        arrived(rb.at[i], m.sib_r.at[e, i])
+        pair[i, c] = (pair[i, c].astype(F32) + rb[i].astype(F32)).astype(BF16)
+        if e in (0, 2):
+            ex_open[e, i].append(push(pair.at[i, c], rx.at[i], m.xs.at[e, i], m.xr.at[e, i], nbr, keep=False))
+        else:
+            copy = remote(pair.at[i, c], rx.at[i // 2], m.xs.at[e, i], m.xr.at[e, i // 2], nbr)
+            far = p != i % 2
+
+            @pl.when(far)
+            def _():
+                copy.start()
+
+            ex_far[e].append((jnp.logical_not(far), copy))
+
+    def ex_close(e, i):
+        for copy in ex_open[e, i]:
+            copy.wait_send()
+        ex_open[e, i] = []
+
+    def ex_total(e, i):
+        pair, _, rx = EX[e]
+        arrived(rx.at[i], m.xr.at[e, i])
+        return pair[i, c].astype(F32) + rx[i].astype(F32)
+
+    PS = (m.P0, m.P1, m.P2, m.P3)
+
+    def attend(i):
+        span = (i + 1) * rows
+        r0 = i * rows
+        start = m.ST[i, 0][0:1, 0:1].astype(F32)
+        for j in range(2):
+            q = m.QKV[r0 : r0 + rows, j * hd : (j + 1) * hd]
+            k = m.QKV[0:span, two + j * hd : two + (j + 1) * hd]
+            s = dot_nt(q, k) * scale
+            row = lax.broadcasted_iota(jnp.int32, (rows, span), 0) + r0
+            col = lax.broadcasted_iota(jnp.int32, (rows, span), 1)
+            s = jnp.where((col <= row) & (col.astype(F32) >= start), s, masked_value)
+            e = jnp.exp(s - jnp.max(s, axis=-1, keepdims=True))
+            p = (e * (1.0 / jnp.sum(e, axis=-1, keepdims=True))).astype(BF16)
+            PS[i][j] = p
+            v = m.QKV[0:span, 2 * two + j * hd : 2 * two + (j + 1) * hd]
+            m.MIX[r0 : r0 + rows, j * hd : (j + 1) * hd] = dot_nn(p, v).astype(BF16)
+
+        @pl.loop(0, 4)
+        def _(n):
+            w = m.WO[:, :, :, :, col_tile(n)].reshape(two, 256)
+            ex_put(0, i, col_tile(n), dot_nn(m.MIX[r0 : r0 + rows, :], w))
+
+        ex_send(0, i)
+
+    def second_norm(i):
+        res = m.X[i, c].astype(F32) + ex_total(0, i)
+        m.RES[i] = res
+        xhat, _ = norm_parts(res)
+        m.N2[i, c] = (xhat * m.VF[3:4] + m.VF[4:5]).astype(BF16)
+        push(m.N2.at[i, c], m.N2.at[i, c], m.n2_s.at[i], m.n2_r.at[i], sib)
+
+    m.VSUM[...] = jnp.zeros((8, width), F32)
+
+    def feed(n):
+        tile = col_tile(n)
+        w_in = m.WU[:, :, :, :, tile].reshape(width, 256)
+        w_back = m.WD[pl.ds(n * (256 // fw), 256 // fw)].reshape(256, width)
+
+        @pl.loop(0, 4)
+        def _(i):
+            pre = dot_nn(m.N2[i].reshape(rows, width), w_in) + m.VF[5:6, tile]
+            back = dot_nt(m.DZ[i].reshape(rows, width), w_back)
+            sq = pre * pre
+            th = jnp.tanh(GELU_K * pre * (1.0 + GELU_C * sq))
+            m.HID[row_tile(i), tile] = (0.5 * pre * (1.0 + th)).astype(BF16)
+            slope = 0.5 * (1.0 + th) + 0.5 * pre * (1.0 - th * th) * (GELU_K * (1.0 + 3.0 * GELU_C * sq))
+            dpre = back * slope
+            m.VSUM[5:6, tile] += jnp.sum(dpre, axis=0, keepdims=True)
+            m.DP[row_tile(i), tile] = dpre.astype(BF16)
+
+    def feed_two(i):
+        r0 = i * rows
+        ex_close(0, i)
+
+        @pl.loop(0, width // 256)
+        def _(n):
+            w = m.WU[n].reshape(256, hid)
+            ex_put(2, i, col_tile(n), dot_nt(m.DP[r0 : r0 + rows, :], w))
+
+        ex_send(2, i)
+
+    def feed_out(i):
+        r0 = i * rows
+
+        @pl.loop(0, width // 256)
+        def _(n):
+            w = m.WD[:, :, col_tile(n)].reshape(hid, 256)
+            ex_put(1, i, col_tile(n), dot_nn(m.HID[r0 : r0 + rows, :], w))
+
+        ex_send(1, i)
+
+    def feed_back(i):
+        xhat, rstd = norm_parts(m.RES[i])
+        g = ex_total(2, i)
+        a = 0.5 * jnp.sum(g * xhat, axis=0, keepdims=True)
+        b = 0.5 * jnp.sum(g, axis=0, keepdims=True)
+        m.VSUM[3:4] += a
+        m.VSUM[4:5] += b
+
+        @pl.when(p == i % 2)
+        def _():
+            m.KEEP[i // 2] = m.RES[i]
+
+        dres = m.DZ[i, c].astype(F32) + norm_back(g, m.VF[3:4], xhat, rstd)
+        m.RES[i] = dres
+        m.DB[i, c] = dres.astype(BF16)
+        push(m.DB.at[i, c], m.DB.at[i, c], m.db_s.at[i], m.db_r.at[i], sib)
+
+    def lane(ref, at):
+        return ref[:, pl.ds(pl.multiple_of(at * 128, 128), 128)]
+
+    def lane_n2(at):
+        return m.N2[:, :, :, pl.ds(pl.multiple_of(at * 128, 128), 128)].reshape(4 * rows, 128)
+
+    def flip(parts):
+        for a, part in enumerate(parts):
+            m.TT[a * 128 : (a + 1) * 128, :] = part.T
+
+    SEND = (m.YSF.at[0], m.YSF.at[1], m.YSQ.at[0], m.YSQ.at[1])
+    GOT1 = (m.R1F.at[0], m.R1F.at[1], m.R1Q.at[0], m.R1Q.at[1])
+    GOT2 = (m.R2F.at[0], m.R2F.at[1], m.R2Q.at[0], m.R2Q.at[1])
+    GOT3 = (m.R3F.at[0], m.R3F.at[1], m.R3Q.at[0], m.R3Q.at[1])
+    AXES = ("yx", "xy", "yx", "xy")
+    open1 = {0: [], 1: [], 2: [], 3: []}
+    fh = fw // 2
+
+    def step1(w, slots):
+        for k in slots:
+            open1[w].append(
+                push(SEND[w].at[k], GOT1[w].at[k], m.r1_s.at[w, k], m.r1_r.at[w, k], over[AXES[w][0]], keep=False)
+            )
+
+    def up_lhs(yy):
+        flip([lane_n2((yy * 2 + a // 2) * 2 + a % 2) for a in range(4)])
+
+    def up_parts(res):
+        return [
+            ((a // 2) * 2 + b, (a % 2) * fh, res[a * 128 + b * fh : a * 128 + (b + 1) * fh])
+            for a in range(4)
+            for b in range(2)
+        ]
+
+    def far_tile(k):
+        return 2 * k + 1 - x if k < 2 else 2 * (k - 2) + x
+
+    def up_far(k):
+        s = col_tile(far_tile(k))
+        for slot, at, part in up_parts(dot_nn(m.TT[...], m.DP[:, s])):
+            m.YSF[0, slot, at : at + fh, s] = part.astype(BF16)
+        for slot in range(4):
+            src, dst = m.YSF.at[0, slot, :, s], m.R1F.at[0, slot, :, s]
+            open1[0].append(push(src, dst, m.up_s.at[k, slot], m.up_r.at[k, slot], over["y"], keep=False))
+
+    def down_far(k):
+        for a in range(2):
+            m.TU[a * 128 : (a + 1) * 128, :] = lane(m.HID, far_tile(k) * 2 + a).T
+
+        @pl.loop(0, width // 256)
+        def _(n):
+            s = col_tile(n)
+            res = dot_nn(m.TU[...], m.DZ[:, :, :, s].reshape(4 * rows, 256)).astype(BF16)
+            m.YSF[1, 2 * k, :, s] = res[0:fw]
+            m.YSF[1, 2 * k + 1, :, s] = res[fw : 2 * fw]
+
+        step1(1, (2 * k, 2 * k + 1))
+
+    def qkv_lhs(yy, xx):
+        flip([lane(m.N1, (yy * 2 + a) * 2) for a in range(2)] + [lane(m.N1, (a * 2 + xx) * 2 + 1) for a in range(2)])
+
+    def qkv_parts(res):
+        return [
+            (a // 2, (a % 2) * 2 + b, res[a * 128 + b * fh : a * 128 + (b + 1) * fh]) for a in range(4) for b in range(2)
+        ]
+
+    def qkv_far():
+        qkv_lhs(1 - y, 1 - x)
+
+        @pl.loop(0, 3)
+        def _(n):
+            s = col_tile(n)
+            for e, slot, part in qkv_parts(dot_nn(m.TT[...], m.QKV[:, s])):
+                m.YSQ[e, slot, :, s] = part.astype(BF16)
+
+        step1(2, range(4))
+        step1(3, range(4))
+
+    def near_wait(w):
+        for copy in open1[w]:
+            copy.wait_send()
+        for slot in range(4):
+            if w:
+                arrived(GOT1[w].at[slot], m.r1_r.at[w, slot])
+            else:
+                for k in range(4):
+                    arrived(m.R1F.at[0, slot, :, col_tile(far_tile(k))], m.up_r.at[k, slot])
+
+    def step2(w):
+        first, second = AXES[w]
+        there = 1 - (x if second == "x" else y)
+        for qq in range(2):
+            push(
+                SEND[w].at[there * 2 + qq], GOT2[w].at[qq], m.r2_s.at[w, qq], m.r2_r.at[w, qq], over[second]
+            )
+
+    def up_near():
+        up_lhs(y)
+        near_wait(0)
+
+        @pl.loop(0, hid // 256)
+        def _(n):
+            s = col_tile(n)
+            for slot, at, part in up_parts(dot_nn(m.TT[...], m.DP[:, s])):
+                to = slice(at, at + fh)
+                m.YSF[0, slot, to, s] = (part + m.R1F[0, slot, to, s].astype(F32)).astype(BF16)
+
+        step2(0)
+
+    def down_near():
+        near_wait(1)
+        for k in range(2):
+            for a in range(2):
+                m.TU[a * 128 : (a + 1) * 128, :] = lane(m.HID, far_tile(k + 2) * 2 + a).T
+
+            @pl.loop(0, width // 256)
+            def _(n):
+                s = col_tile(n)
+                res = dot_nn(m.TU[...], m.DZ[:, :, :, s].reshape(4 * rows, 256))
+                for b in range(2):
+                    got = m.R1F[1, 2 * k + b, :, s].astype(F32)
+                    m.YSF[1, 2 * k + b, :, s] = (res[b * fw : (b + 1) * fw] + got).astype(BF16)
+
+        step2(1)
+
+    def qkv_near():
+        qkv_lhs(y, x)
+        near_wait(2)
+        near_wait(3)
+
+        @pl.loop(0, 3)
+        def _(n):
+            s = col_tile(n)
+            for e, slot, part in qkv_parts(dot_nn(m.TT[...], m.QKV[:, s])):
+                m.YSQ[e, slot, :, s] = (part + m.R1Q[e, slot, :, s].astype(F32)).astype(BF16)
+
+        step2(2)
+        step2(3)
+
+    def here(w):
+        return x if AXES[w][1] == "x" else y
+
+    def grad_mid(w):
+        for qq in range(2):
+            arrived(GOT2[w].at[qq], m.r2_r.at[w, qq])
+            slot = here(w) * 2 + qq
+            SEND[w][slot] = (SEND[w][slot].astype(F32) + GOT2[w][qq].astype(F32)).astype(BF16)
+        push(SEND[w].at[here(w) * 2 + 1 - q], GOT3[w], m.r3_s.at[w], m.r3_r.at[w], over["q"])
+
+    def grad_sum(w):
+        arrived(GOT3[w], m.r3_r.at[w])
+        return SEND[w][here(w) * 2 + q].astype(F32) + GOT3[w][...].astype(F32)
+
+    def out_first():
+        flip([lane(m.MIX, a) for a in range(2)])
+
+        @pl.loop(0, width // 256)
+        def _(n):
+            s = col_tile(n)
+            res = dot_nn(m.TT[0:two, :], m.DB[:, :, :, s].reshape(4 * rows, 256)).astype(BF16)
+            m.GOB[:, :, :, :, s] = res.reshape(2, 2, 2, rw, 256)
+
+        for yy in range(2):
+            for qq in range(2):
+                k = yy * 2 + qq
+                push(m.GOB.at[yy, qq, 1 - p], m.GOR.at[yy, qq], m.sw_s2.at[k], m.sw_r2.at[k], nbr)
+
+    def out_second():
+        for yy in range(2):
+            for qq in range(2):
+                arrived(m.GOR.at[yy, qq], m.sw_r2.at[yy * 2 + qq])
+                m.GOS[at8(yy, p, qq)] = m.GOB[yy, qq, p]
+                m.GOS[at8(yy, 1 - p, qq)] = m.GOR[yy, qq]
+        for k, f in enumerate(flips):
+            if k:
+                spot = flipped(*f)
+                push(m.GOS.at[at8(*spot)], m.GOT.at[me], m.go_s.at[k], m.go_r.at[me], peer(*spot))
+
+    def out_sum():
+        value = m.GOS[me].astype(F32)
+        for k, f in enumerate(flips):
+            if k:
+                at = at8(*flipped(*f))
+                arrived(m.GOT.at[at], m.go_r.at[at])
+                value = value + m.GOT[at].astype(F32)
+        m.OO[...] = value
+
+    def give(e, src_of, dst):
+        pltpu.make_async_copy(src_of(c, p), dst.at[t], m.pe_r.at[e, t]).start()
+        for d in (1, 2, 3):
+            tt = lax.rem(t + d, 4)
+            push(src_of(lax.rem(tt, 2), lax.div(tt, 2)), dst.at[t], m.pe_s.at[e, d - 1], m.pe_r.at[e, t], mate(tt))
+
+    def give_end():
+        for e, dst in ((0, m.peu), (1, m.peq)):
+            for tt in range(4):
+                arrived(dst.at[tt], m.pe_r.at[e, tt])
+
+    swap_out()
+    gather_pass(FFN, 0)
+    swap_end()
+    attend(0)
+    attend(1)
+    ex_mid(0, 0)
+    gather_pass(FFN, 1)
+    attend(2)
+    ex_mid(0, 1)
+    second_norm(0)
+    attend(3)
+    ex_mid(0, 2)
+    second_norm(1)
+    ex_mid(0, 3)
+    gather_pass(FFN, 2)
+    spread_own(2)
+    second_norm(2)
+    second_norm(3)
+    spread_nbr(2)
+    for i in range(4):
+        arrived(m.N2.at[i, 1 - c], m.n2_r.at[i])
+    up_lhs(1 - y)
+    spread_end(2)
+    gather_end(FFN)
+    for k in range(4):
+        feed(far_tile(k))
+        if k < 2:
+            down_far(k)
+        up_far(k)
+    for i in range(4):
+        feed_two(i)
+        if i:
+            ex_mid(2, i - 1)
+    ex_mid(2, 3)
+    for i in range(4):
+        feed_out(i)
+    feed_back(0)
+    feed_back(1)
+    for i in range(4):
+        ex_mid(1, i)
+
+    def attend_back(i):
+        arrived(m.DB.at[i, 1 - c], m.db_r.at[i])
+        span = (i + 1) * rows
+        r0 = i * rows
+        m.DMIX[...] = dot_nt(m.DB[i].reshape(rows, width), m.WO[...].reshape(two, width)).astype(BF16)
+        for j in range(2):
+            k0, v0 = two + j * hd, 2 * two + j * hd
+            do = m.DMIX[:, j * hd : (j + 1) * hd]
+            p = PS[i][j]
+            pf = p.astype(F32)
+            g = dot_nt(do, m.QKV[0:span, v0 : v0 + hd])
+            delta = jnp.sum(pf * g, axis=-1, keepdims=True)
+            ds = (pf * (g - delta) * scale).astype(BF16)
+            q = m.QKV[r0 : r0 + rows, j * hd : (j + 1) * hd]
+            dk = dot_tn(ds, q)
+            dv = dot_tn(p, do)
+            dq = dot_nn(ds, m.QKV[0:span, k0 : k0 + hd])
+            ka, va = slice(j * hd, (j + 1) * hd), slice(two + j * hd, two + (j + 1) * hd)
+            if i:
+                m.ACC[0:r0, ka] += dk[0:r0]
+                m.ACC[0:r0, va] += dv[0:r0]
+            m.ACC[r0:span, ka] = dk[r0:span]
+            m.ACC[r0:span, va] = dv[r0:span]
+            m.QKV[r0 : r0 + rows, j * hd : (j + 1) * hd] = dq.astype(BF16)
+
+    def give_back(k, kk, buf, dst):
+        i = mine[kk]
+        near = (q == c) & (i == z)
+        to = dst.at[pl.ds(pl.multiple_of(c * half, half), half)]
+        rsem = m.ret_r.at[k, c]
+
+        @pl.when(near)
+        def _():
+            pltpu.make_async_copy(buf.at[kk], to, rsem).start()
+
+        copy = remote(buf.at[kk], to, m.ret_s.at[k, kk], rsem, dev(y, x, q, i))
+
+        @pl.when(jnp.logical_not(near))
+        def _():
+            copy.start()
+
+        homes.append((near, copy))
+
+    def far_close(e):
+        for near, copy in ex_far.pop(e):
+
+            @pl.when(jnp.logical_not(near))
+            def _():
+                copy.wait_send()
+
+    def finish_out(kk):
+        i = mine[kk]
+        arrived(m.RXb.at[kk], m.xr.at[1, kk])
+        value = m.KEEP[kk] + m.PR1[i, c].astype(F32) + m.RXb[kk].astype(F32) + m.VF[0:1]
+        m.OUTB[kk] = value.astype(BF16)
+        give_back(0, kk, m.OUTB, m.out)
+
+    def first_back(i):
+        r0 = i * rows
+
+        @pl.loop(0, width // 256)
+        def _(n):
+            w = m.WA[n].reshape(256, cols)
+            ex_put(3, i, col_tile(n), dot_nt(m.QKV[r0 : r0 + rows, :], w))
+
+        ex_send(3, i)
+
+    def finish_in(kk):
+        i = mine[kk]
+        arrived(m.RXd.at[kk], m.xr.at[3, kk])
+        g = m.PR1[i, c].astype(F32) + m.RXd[kk].astype(F32)
+        xhat, rstd = norm_parts(m.X[i, c].astype(F32))
+        parts = (
+            jnp.sum(m.DZ[i, c].astype(F32), axis=0, keepdims=True),
+            jnp.sum(g * xhat, axis=0, keepdims=True),
+            jnp.sum(g, axis=0, keepdims=True),
+        )
+        for k, part in enumerate(parts):
+            m.VSUM[k : k + 1] += part
+        m.IGB[kk] = (m.RES[i] + norm_back(g, m.VF[1:2], xhat, rstd)).astype(BF16)
+        give_back(1, kk, m.IGB, m.ig)
+
+    attend_back(0)
+    feed_back(2)
+    attend_back(1)
+    feed_back(3)
+    finish_out(0)
+    finish_out(1)
+    attend_back(2)
+    down_near()
+    attend_back(3)
+
+    @pl.loop(0, 4)
+    def _(i):
+        m.QKV[row_tile(i), two : 3 * two] = m.ACC[row_tile(i), :].astype(BF16)
+
+    qkv_far()
+    out_first()
+    up_near()
+    far_close(1)
+    for i in range(4):
+        ex_close(1, i)
+    for i in range(4):
+        first_back(i)
+        if i:
+            ex_mid(3, i - 1)
+    grad_mid(1)
+    ex_mid(3, 3)
+    out_second()
+    grad_mid(0)
+    finish_in(0)
+    finish_in(1)
+
+    for d in (1, 2, 3):
+        tt = lax.rem(t + d, 4)
+        push(m.VSUM, m.VR1.at[t], m.v1_s.at[d - 1], m.v1_r.at[t], mate(tt))
+    qkv_near()
+    rest = m.VSUM[...]
+    for d in (1, 2, 3):
+        tt = lax.rem(t + d, 4)
+        arrived(m.VR1.at[tt], m.v1_r.at[tt])
+        rest = rest + m.VR1[tt]
+    row8 = lax.broadcasted_iota(jnp.int32, (8, width), 0)
+    m.VMID[...] = jnp.where(row8 == 5, m.VSUM[...], rest)
+    for k, f in enumerate(flips):
+        if k:
+            push(m.VMID, m.VR2.at[me], m.v2_s.at[k - 1], m.v2_r.at[me], peer(*flipped(*f)))
+    m.OD[...] = grad_sum(1)
+    keep_down = pltpu.make_async_copy(m.OD, m.gdn, m.loc.at[2])
+    keep_down.start()
+    m.FIU[...] = grad_sum(0).astype(BF16)
+    give(0, lambda cc, pp: m.FIU.at[pl.ds(pl.multiple_of((cc * 2 + pp) * rw, rw), rw)], m.peu)
+    grad_mid(2)
+    grad_mid(3)
+    out_sum()
+    keep_out = pltpu.make_async_copy(m.OO, m.go, m.loc.at[3])
+    keep_out.start()
+    for e in range(2):
+        m.FIN[e] = grad_sum(2 + e).astype(BF16)
+    give(1, lambda cc, pp: m.FIN.at[cc, pl.ds(pl.multiple_of(pp * rw, rw), rw)], m.peq)
+    final = m.VMID[...]
+    for k, f in enumerate(flips):
+        if k:
+            at = at8(*flipped(*f))
+            arrived(m.VR2.at[at], m.v2_r.at[at])
+            final = final + m.VR2[at]
+    m.gvec[...] = final
+
+    for k, dst in enumerate((m.out, m.ig)):
+        for cc in range(2):
+            arrived(dst.at[pl.ds(cc * half, half)], m.ret_r.at[k, cc])
+    give_end()
+    keep_down.wait()
+    keep_out.wait()
+    for copy in sent:
+        copy.wait_send()
+    for e, i in ex_open:
+        ex_close(e, i)
+    far_close(3)
+    for near, copy in homes:
+
+        @pl.when(jnp.logical_not(near))
+        def _():
+            copy.wait_send()
+
+
+def place_outputs(out_i, ig_i, peq, peu, go_i, gdn_i, out, ig, gq, gk, gv, go, gup, gdn, PQ, PU, GQ, GU, A, B, GO, GD, sem):
+    pairs = ((peq, PQ), (peu, PU), (out_i, A), (ig_i, B), (go_i, GO), (gdn_i, GD))
+    moves = [pltpu.make_async_copy(src, dst, sem.at[k]) for k, (src, dst) in enumerate(pairs)]
+    for move in moves:
+        move.start()
+    results = ((A, out), (B, ig), (GO, go), (GD, gdn), (GQ.at[0], gq), (GQ.at[1], gk), (GQ.at[2], gv), (GU, gup))
+    last = [pltpu.make_async_copy(src, dst, sem.at[6 + k]) for k, (src, dst) in enumerate(results)]
+    hd = PQ.shape[2] // 6
+    fw = PU.shape[2] // 8
+    moves[0].wait()
+    moves[1].wait()
+    for tt in range(RANKS):
+        for j in range(2):
+            a = (j * RANKS + tt) * hd
+            for n in range(3):
+                GQ[n, :, a : a + hd] = PQ[tt, :, (n * 2 + j) * hd : (n * 2 + j + 1) * hd].astype(F32)
+        for k in range(8):
+            a = hidden_at(k, tt) * fw
+            GU[:, a : a + fw] = PU[tt, :, k * fw : (k + 1) * fw].astype(F32)
+    for k in range(4):
+        last[4 + k].start()
+    for k in range(4):
+        moves[2 + k].wait()
+        last[k].start()
+    for move in last:
+        move.wait()
+
+
+def call_fused(inputs, positions, w_query, w_key, w_value, w_out, w_up, w_down, up_bias, down_bias,
+               ln1_gain, ln1_bias, ln2_gain, ln2_bias, cotangent):
+    rows, width = inputs.shape
+    hid = w_up.shape[1] // RANKS
+    rw, fw = w_query.shape[0], w_down.shape[0]
+    shapes = scratch_of(rows, width, hid, rw, fw)
+    dp, blk = lax.axis_index("dp"), lax.axis_index("blk")
+    n_blk = lax.axis_size("blk")
+    place = dp * n_blk + blk
+    at_up = dp // 2 * 2 + blk // 2
+    small_in = [v.reshape(1, -1) for v in (down_bias, ln1_gain, ln1_bias, ln2_gain, ln2_bias, up_bias)]
+    names = IN_NAMES + OUT_NAMES + tuple(shapes)
+    any_, vm = pl.BlockSpec(memory_space=pl.ANY), pl.BlockSpec(memory_space=pltpu.VMEM)
+    S = jax.ShapeDtypeStruct
+    cols = 3 * 2 * (width // HEADS)
+    tokens, wide = S((rows, width), BF16), S((rw, width), F32)
+    moved = (S((RANKS, rw, cols), BF16), S((RANKS, rw, hid), BF16))
+    out, ig, peq, peu, go, gdn, gvec = pl.pallas_call(
+        functools.partial(fused, names),
+        out_shape=(tokens, tokens) + moved + (wide, S(w_down.shape, F32), S((8, width), F32)),
+        in_specs=[any_, any_, vm] + [any_] * 6 + [vm] * 6,
+        out_specs=[any_] * 6 + [vm],
+        scratch_shapes=list(shapes.values()),
+        compiler_params=pltpu.CompilerParams(
+            collective_id=0, has_side_effects=True, vmem_limit_bytes=VMEM_BYTES
+        ),
+        cost_estimate=pl.CostEstimate(flops=23 * 10**9, bytes_accessed=10**7, transcendentals=10**6),
+    )(inputs, cotangent, positions.reshape(2, -1), w_query, w_key, w_value, w_out, w_up, w_down, *small_in)
+    out, ig, gq, gk, gv, go, gup, gdn = pl.pallas_call(
+        place_outputs,
+        out_shape=(tokens, tokens, wide, wide, wide, wide, S(w_up.shape, F32), S(w_down.shape, F32)),
+        in_specs=[any_] * 6,
+        out_specs=[any_] * 8,
+        scratch_shapes=[
+            pltpu.VMEM(moved[0].shape, BF16),
+            pltpu.VMEM(moved[1].shape, BF16),
+            pltpu.VMEM((3, rw, width), F32),
+            pltpu.VMEM(w_up.shape, F32),
+            pltpu.VMEM((rows, width), BF16),
+            pltpu.VMEM((rows, width), BF16),
+            pltpu.VMEM((rw, width), F32),
+            pltpu.VMEM(w_down.shape, F32),
+            pltpu.SemaphoreType.DMA((14,)),
+        ],
+        compiler_params=pltpu.CompilerParams(vmem_limit_bytes=VMEM_BYTES),
+    )(out, ig, peq, peu, go, gdn)
+    small = lax.dynamic_slice(gvec, (0, place * rw), (5, rw))
+    gup_bias = lax.dynamic_slice(gvec, (5, at_up * fw), (1, fw))[0]
+    return (out, ig, gq, gk, gv, go, gup, gdn, gup_bias, small[0], small[1], small[2], small[3], small[4])
 
 
 def layer_norm(values, gain, offset):
@@ -311,4 +1410,13 @@
         P(("dp", "blk")),
         P(("dp", "blk")),
     )
-    return jax.shard_map(local, mesh=mesh, in_specs=in_specs, out_specs=out_specs, check_vma=False)
+    n_dp, n_blk = mesh.shape["dp"], mesh.shape["blk"]
+
+    def layer(*args):
+        fits = n_blk == RANKS and n_dp == 2 * RANKS and args[2].shape[0] // (n_dp * n_blk) % 16 == 0
+        call = jax.shard_map(
+            call_fused if fits else local, mesh=mesh, in_specs=in_specs, out_specs=out_specs, check_vma=False
+        )
+        return call(*args)
+
+    return layer

time: 1990 us -> 258 us (0.13)
  waiting for transfers between devices: 1650 us -> 0 us
  Pallas kernels: 0 us -> 252 us
  blocking collectives: 150 us -> 0 us
  matrix products: 101 us -> 0 us
  local copies, waits for them, and re-layouts: 28.9 us -> 2.53 us
    reduce_scatter x7 -> x0, waiting for transfers between devices: 1330 us -> none  [the longest x1 366 us: local(): lax.psum_scatter(grad_up_w, ('dp', 'blk'), scatter_dimension=0, tiled=True)]
    all_gather x8 -> x0, waiting for transfers between devices: 319 us -> none  [the longest x1 76.3 us: local(): lax.all_gather(w_down, ('dp', 'blk'), axis=0, tiled=True)]
    pallas_call x0 -> x2, Pallas kernels: none -> 252 us  [the longest x1 250 us: call_fused(): pl.pallas_call(functools.partial(fused, names), out_shape=(tokens, tokens...]
    dot_general x27 -> x0, matrix products: 101 us -> none  [the longest x1 11.6 us: local(): jnp.dot(normed_two, ffn_full[0], preferred_element_type=jnp.float32)]
    unnamed x2 -> x0, blocking collectives: 84.5 us -> none
    all_gather x1 -> x0, blocking collectives: 66 us -> none  [local(): lax.all_gather(up_bias, ('dp', 'blk'), axis=0, tiled=True)]
  transfers between devices with their start and end apart: 15 -> 0, of which waited for: 14 -> 0; matrix products, arithmetic and copies ran while one was open for 5% -> 0% of each run, Pallas kernels for 0% -> 0%
where the time goes in v1:
time: 258 us; the launch traced here: 256 us
  Pallas kernels  252 us (98%)
    pallas_call x1, Pallas kernels, call_fused(): pl.pallas_call(functools.partial(fused, names), out_shape=(tokens, tokens...  250 us

profile of v1, /device:TPU:0, one launch (start us, length us, event | category | flops | bytes accessed | tf_op | source)
XLA Modules:
  0.0 255.9 jit_solution(9316667528562793646)
XLA Ops:
  0.7 249.7 %shard_map.254 = (bf16[256,1024]{1,0:T(8,128)(2,1)}, bf16[256,1024]{1,0:T(8,128)(2,1)}, bf16[4,32,768]{2,1,0:T(8,128)(2,1)}, bf16[4,32,1024]{2,1,0:T(8,128)(2,1)...) custom-call(bf16[256,1024]{1,0:T(8,128)(2,1)} %all_refs_0_.1, bf16[256,1024]{1,0:T(8,128)(2,1)} %all_refs_1_.1, ...), custom_call_target="tpu_custom_call" | custom-call | flops 23000000512 | bytes 10000000 | tf_op jit(solution)/shard_map/pallas_call | solution.py:1080
  250.4 1.3 dynamic-slice_bitcast_fusion
  251.7 0.7 constant_dynamic-slice_fusion
  252.4 0.5 slice_bitcast_fusion
  253.0 2.7 %shard_map.255 = (bf16[256,1024]{1,0:T(8,128)(2,1)}, bf16[256,1024]{1,0:T(8,128)(2,1)}, f32[32,1024]{1,0:T(8,128)}, f32[32,1024]{1,0:T(8,128)}, f32[32,1024]{1,0...) custom-call(bf16[256,1024]{1,0:T(8,128)(2,1)} %get-tuple-element.29.out_i, ...), custom_call_target="tpu_custom_call" | custom-call | tf_op jit(solution)/shard_map/pallas_call | solution.py:1091

commit v2 on v1

--- a/solution.py
+++ b/solution.py
@@ -282,47 +282,54 @@
     )
     to_z = 2 * c + p
 
-    def spread_home(k):
+    def spread_home(k, stays):
         src, buf = streams[k]
         for cc in range(2):
-            own = (q == c) & (c == cc)
             dst = buf.at[z, cc]
             rsem = m.sp_r.at[k, z, cc]
-
-            @pl.when(own)
-            def _():
-                pltpu.make_async_copy(src(cc), dst, rsem).start()
-
             copy = remote(src(cc), dst, m.sp_s.at[k, cc], rsem, dev(y, x, cc, to_z))
-
-            @pl.when(jnp.logical_not(own))
-            def _():
-                copy.start()
-
-            homes.append((own, copy))
-
-    def spread_own(k):
+            if stays:
+
+                @pl.when((q == c) & (c == cc))
+                def _():
+                    pltpu.make_async_copy(src(cc), dst, rsem).start()
+
+                @pl.when((q == c) & (c != cc))
+                def _():
+                    copy.start()
+
+                homes.append(((q == c) & (c == cc), copy))
+            else:
+
+                @pl.when(q != c)
+                def _():
+                    copy.start()
+
+    held = (z, lax.rem(z + 2, 4))
+    beside = (2 * q + 1 - p, lax.rem(2 * q + 3 - p, 4))
+
+    def spread_own(k, far):
         _, buf = streams[k]
-        for kk in range(2):
-            i = mine[kk]
-            arrived(buf.at[i, c], m.sp_r.at[k, i, c])
-            push(buf.at[i, c], buf.at[i, c], m.sp_s.at[k, 2 + 2 * kk], m.sp_r.at[k, i, c], nbr)
-            push(buf.at[i, c], buf.at[i, c], m.sp_s.at[k, 3 + 2 * kk], m.sp_r.at[k, i, c], sib)
-
-    def spread_nbr(k):
+        i = held[far]
+        arrived(buf.at[i, c], m.sp_r.at[k, i, c])
+        push(buf.at[i, c], buf.at[i, c], m.sp_s.at[k, 2 + 2 * far], m.sp_r.at[k, i, c], nbr)
+        push(buf.at[i, c], buf.at[i, c], m.sp_s.at[k, 3 + 2 * far], m.sp_r.at[k, i, c], sib)
+
+    def spread_nbr(k, far):
         _, buf = streams[k]
-        for kk in range(2):
-            j = theirs[kk]
-            arrived(buf.at[j, c], m.sp_r.at[k, j, c])
-            push(buf.at[j, c], buf.at[j, c], m.sp_s.at[k, 6 + kk], m.sp_r.at[k, j, c], sib)
+        j = beside[far]
+        arrived(buf.at[j, c], m.sp_r.at[k, j, c])
+        push(buf.at[j, c], buf.at[j, c], m.sp_s.at[k, 6 + far], m.sp_r.at[k, j, c], sib)
 
     def spread_end(k):
         _, buf = streams[k]
-        for i in mine + theirs:
+        for i in held + beside:
             arrived(buf.at[i, 1 - c], m.sp_r.at[k, i, 1 - c])
 
-    spread_home(0)
-    spread_home(1)
+    for k in range(2):
+        spread_home(k, False)
+        spread_home(k, True)
+    spread_home(2, True)
 
     for copy in loads:
         copy.wait()
@@ -353,12 +360,16 @@
         return (m.WA if n == 0 else m.WU).at[rank_rows(lax.rem(tt, 2), lax.div(tt, 2))]
 
     pre_sent = []
-    for n in (1, 0, 2):
+
+    def pre_send(n):
         for d in (1, 2, 3):
             tt = lax.rem(t + d, 4)
             pre_sent.append(
                 push(pre_src(n, tt), pre_dst(n, t), m.pre_s.at[n, d - 1], m.pre_r.at[n, t], mate(tt), keep=False)
             )
+
+    pre_send(1)
+    pre_send(0)
     local_o = pltpu.make_async_copy(m.wo, m.WOP.at[me], m.loc.at[0])
     local_o.start()
     local_d = pltpu.make_async_copy(m.wdn, m.WD.at[me], m.loc.at[1])
@@ -389,8 +400,8 @@
         ref = piece(n, *spot)
         push(ref, ref, m.ag_s.at[n, k], m.ag_r.at[n, at8(*spot)], over[to])
 
-    def gather_own(group):
-        for k in range(3):
+    def gather_own(group, steps=(0, 1, 2)):
+        for k in steps:
             for n in group:
                 gather_send(n, (y, x, q), k, ("q" + order(n))[k])
 
@@ -420,48 +431,20 @@
         at = pl.ds(pl.multiple_of(i * rows + h * half, half), half)
         m.N1[at, :] = (xhat * m.VF[1:2] + m.VF[2:3]).astype(BF16)
 
-    pre_wait(1)
-    total = sum((m.PV[a].astype(F32) for a in range(1, 4)), m.PV[0].astype(F32))
-    line = lax.broadcasted_iota(jnp.int32, (16, width), 0)
-    own_vec = jnp.where(line == 5, m.vec[...].astype(F32), total)
-    m.VEC[me] = own_vec.astype(BF16)
-    gather_own(VECS)
-    pre_wait(0)
-    gather_own(ATT)
-    local_o.wait()
-    local_d.wait()
-    pre_wait(2)
-    for copy in pre_sent:
-        copy.wait_send()
-    gather_pass(VECS, 0)
-    gather_pass(VECS, 1)
-    gather_pass(VECS, 2)
-    spread_own(0)
-    spread_own(1)
-    gather_pass(ATT, 0)
-    gather_own(WOUT)
-    gather_own(FFN)
-    gather_end(VECS)
-    every = m.VEC[0].astype(F32)
-    for a in range(1, 8):
-        every = every + m.VEC[a].astype(F32)
-    m.VF[...] = every[0:8]
-    for i in mine:
-        norm_one(i, c)
-    gather_pass(ATT, 1)
-    spread_nbr(0)
-    spread_nbr(1)
-    gather_pass(ATT, 2)
-    spread_home(2)
-    for i in theirs:
-        norm_one(i, c)
-    spread_end(0)
-    spread_end(1)
-    for i in mine + theirs:
-        norm_one(i, 1 - c)
-    for k in range(3):
-        gather_pass(WOUT, k)
-    gather_end(ATT)
+    def vec_own():
+        pre_wait(1)
+        total = sum((m.PV[a].astype(F32) for a in range(1, 4)), m.PV[0].astype(F32))
+        line = lax.broadcasted_iota(jnp.int32, (16, width), 0)
+        own_vec = jnp.where(line == 5, m.vec[...].astype(F32), total)
+        m.VEC[me] = own_vec.astype(BF16)
+        gather_own(VECS)
+
+    def vec_end():
+        gather_end(VECS)
+        every = m.VEC[0].astype(F32)
+        for a in range(1, 8):
+            every = every + m.VEC[a].astype(F32)
+        m.VF[...] = every[0:8]
 
     def swap_out():
         gather_end(WOUT)
@@ -477,6 +460,49 @@
         for yy in range(2):
             for qq in range(2):
                 arrived(m.WO.at[yy, qq, 1 - p], m.sw_r.at[yy * 2 + qq])
+
+    spread_own(0, 0)
+    spread_own(1, 0)
+    vec_own()
+    pre_wait(0)
+    gather_own(ATT)
+    pre_send(2)
+    local_o.wait()
+    local_d.wait()
+    gather_pass(VECS, 0)
+    gather_own(WOUT)
+    gather_pass(ATT, 0)
+    spread_nbr(0, 0)
+    spread_nbr(1, 0)
+    pre_wait(2)
+    for copy in pre_sent:
+        copy.wait_send()
+    gather_pass(VECS, 1)
+    gather_pass(VECS, 2)
+    gather_own(FFN, (1, 2))
+    vec_end()
+    norm_one(held[0], c)
+    norm_one(beside[0], c)
+    gather_pass(ATT, 1)
+    gather_pass(WOUT, 0)
+    spread_own(2, 0)
+    spread_own(0, 1)
+    spread_own(1, 1)
+    gather_own(FFN, (0,))
+    gather_pass(ATT, 2)
+    norm_one(held[1], c)
+    spread_home(2, False)
+    gather_pass(WOUT, 1)
+    gather_pass(WOUT, 2)
+    spread_nbr(0, 1)
+    spread_nbr(1, 1)
+    swap_out()
+    norm_one(beside[1], c)
+    spread_end(0)
+    spread_end(1)
+    for i in held + beside:
+        norm_one(i, 1 - c)
+    gather_end(ATT)
 
     def row_tile(i):
         return pl.ds(pl.multiple_of(i * rows, rows), rows)
@@ -556,6 +582,9 @@
             v = m.QKV[0:span, 2 * two + j * hd : 2 * two + (j + 1) * hd]
             m.MIX[r0 : r0 + rows, j * hd : (j + 1) * hd] = dot_nn(p, v).astype(BF16)
 
+    def attend_out(i):
+        r0 = i * rows
+
         @pl.loop(0, 4)
         def _(n):
             w = m.WO[:, :, :, :, col_tile(n)].reshape(two, 256)
@@ -797,22 +826,34 @@
     def out_second():
         for yy in range(2):
             for qq in range(2):
-                arrived(m.GOR.at[yy, qq], m.sw_r2.at[yy * 2 + qq])
+                k = yy * 2 + qq
+                arrived(m.GOR.at[yy, qq], m.sw_r2.at[k])
                 m.GOS[at8(yy, p, qq)] = m.GOB[yy, qq, p]
                 m.GOS[at8(yy, 1 - p, qq)] = m.GOR[yy, qq]
-        for k, f in enumerate(flips):
-            if k:
-                spot = flipped(*f)
-                push(m.GOS.at[at8(*spot)], m.GOT.at[me], m.go_s.at[k], m.go_r.at[me], peer(*spot))
+        for yy in range(2):
+            for qq in range(2):
+                k = yy * 2 + qq
+                push(m.GOS.at[at8(yy, 1 - x, qq)], m.GOT.at[k], m.go_s.at[k], m.go_r.at[k], over["x"])
+
+    def out_add(at, k):
+        arrived(m.GOT.at[k], m.go_r.at[k])
+        m.GOS[at] = (m.GOS[at].astype(F32) + m.GOT[k].astype(F32)).astype(BF16)
+
+    def out_third():
+        for yy in range(2):
+            for qq in range(2):
+                out_add(at8(yy, x, qq), yy * 2 + qq)
+        for qq in range(2):
+            push(m.GOS.at[at8(1 - y, x, qq)], m.GOT.at[4 + qq], m.go_s.at[4 + qq], m.go_r.at[4 + qq], over["y"])
+
+    def out_fourth():
+        for qq in range(2):
+            out_add(at8(y, x, qq), 4 + qq)
+        push(m.GOS.at[at8(y, x, 1 - q)], m.GOT.at[6], m.go_s.at[6], m.go_r.at[6], over["q"])
 
     def out_sum():
-        value = m.GOS[me].astype(F32)
-        for k, f in enumerate(flips):
-            if k:
-                at = at8(*flipped(*f))
-                arrived(m.GOT.at[at], m.go_r.at[at])
-                value = value + m.GOT[at].astype(F32)
-        m.OO[...] = value
+        arrived(m.GOT.at[6], m.go_r.at[6])
+        m.OO[...] = m.GOS[me].astype(F32) + m.GOT[6].astype(F32)
 
     def give(e, src_of, dst):
         pltpu.make_async_copy(src_of(c, p), dst.at[t], m.pe_r.at[e, t]).start()
@@ -825,25 +866,29 @@
             for tt in range(4):
                 arrived(dst.at[tt], m.pe_r.at[e, tt])
 
-    swap_out()
+    attend(0)
+    swap_end()
+    attend_out(0)
     gather_pass(FFN, 0)
-    swap_end()
-    attend(0)
     attend(1)
+    attend_out(1)
     ex_mid(0, 0)
+    attend(2)
+    attend_out(2)
     gather_pass(FFN, 1)
-    attend(2)
     ex_mid(0, 1)
     second_norm(0)
     attend(3)
+    attend_out(3)
     ex_mid(0, 2)
+    gather_pass(FFN, 2)
     second_norm(1)
     ex_mid(0, 3)
-    gather_pass(FFN, 2)
-    spread_own(2)
+    spread_nbr(2, 0)
+    spread_own(2, 1)
     second_norm(2)
     second_norm(3)
-    spread_nbr(2)
+    spread_nbr(2, 1)
     for i in range(4):
         arrived(m.N2.at[i, 1 - c], m.n2_r.at[i])
     up_lhs(1 - y)
@@ -863,11 +908,13 @@
         feed_out(i)
     feed_back(0)
     feed_back(1)
-    for i in range(4):
-        ex_mid(1, i)
+    down_near()
+    up_near()
+
+    def db_end(i):
+        arrived(m.DB.at[i, 1 - c], m.db_r.at[i])
 
     def attend_back(i):
-        arrived(m.DB.at[i, 1 - c], m.db_r.at[i])
         span = (i + 1) * rows
         r0 = i * rows
         m.DMIX[...] = dot_nt(m.DB[i].reshape(rows, width), m.WO[...].reshape(two, width)).astype(BF16)
@@ -948,14 +995,23 @@
         m.IGB[kk] = (m.RES[i] + norm_back(g, m.VF[1:2], xhat, rstd)).astype(BF16)
         give_back(1, kk, m.IGB, m.ig)
 
+    db_end(0)
     attend_back(0)
     feed_back(2)
+    db_end(1)
     attend_back(1)
     feed_back(3)
+    for i in range(4):
+        ex_mid(1, i)
+    grad_mid(1)
+    db_end(2)
+    db_end(3)
+    out_first()
+    attend_back(2)
+    grad_mid(0)
     finish_out(0)
     finish_out(1)
-    attend_back(2)
-    down_near()
+    out_second()
     attend_back(3)
 
     @pl.loop(0, 4)
@@ -963,26 +1019,25 @@
         m.QKV[row_tile(i), two : 3 * two] = m.ACC[row_tile(i), :].astype(BF16)
 
     qkv_far()
-    out_first()
-    up_near()
     far_close(1)
     for i in range(4):
         ex_close(1, i)
+    out_third()
     for i in range(4):
         first_back(i)
         if i:
             ex_mid(3, i - 1)
-    grad_mid(1)
     ex_mid(3, 3)
-    out_second()
-    grad_mid(0)
+    out_fourth()
+    qkv_near()
     finish_in(0)
     finish_in(1)
 
     for d in (1, 2, 3):
         tt = lax.rem(t + d, 4)
         push(m.VSUM, m.VR1.at[t], m.v1_s.at[d - 1], m.v1_r.at[t], mate(tt))
-    qkv_near()
+    grad_mid(2)
+    grad_mid(3)
     rest = m.VSUM[...]
     for d in (1, 2, 3):
         tt = lax.rem(t + d, 4)
@@ -998,14 +1053,13 @@
     keep_down.start()
     m.FIU[...] = grad_sum(0).astype(BF16)
     give(0, lambda cc, pp: m.FIU.at[pl.ds(pl.multiple_of((cc * 2 + pp) * rw, rw), rw)], m.peu)
-    grad_mid(2)
-    grad_mid(3)
     out_sum()
     keep_out = pltpu.make_async_copy(m.OO, m.go, m.loc.at[3])
     keep_out.start()
     for e in range(2):
         m.FIN[e] = grad_sum(2 + e).astype(BF16)
     give(1, lambda cc, pp: m.FIN.at[cc, pl.ds(pl.multiple_of(pp * rw, rw), rw)], m.peq)
+
     final = m.VMID[...]
     for k, f in enumerate(flips):
         if k:

time: 258 us -> 247 us (0.957)
  Pallas kernels: 252 us -> 240 us
    pallas_call x1, Pallas kernels: 250 us -> 238 us  [call_fused(): pl.pallas_call(functools.partial(fused, names), out_shape=(tokens, tokens...]
where the time goes in v2:
time: 247 us; the launch traced here: 244 us
  Pallas kernels  240 us (97%)
  local copies, waits for them, and re-layouts  2.53 us (1%)
    pallas_call x1, Pallas kernels, call_fused(): pl.pallas_call(functools.partial(fused, names), out_shape=(tokens, tokens...  238 us

profile of v2, /device:TPU:0, one launch (start us, length us, event | category | flops | bytes accessed | tf_op | source)
XLA Modules:
  0.0 243.6 jit_solution(18248378842695734371)
XLA Ops:
  0.7 237.5 %shard_map.254 = (bf16[256,1024]{1,0:T(8,128)(2,1)}, bf16[256,1024]{1,0:T(8,128)(2,1)}, bf16[4,32,768]{2,1,0:T(8,128)(2,1)}, bf16[4,32,1024]{2,1,0:T(8,128)(2,1)...) custom-call(bf16[256,1024]{1,0:T(8,128)(2,1)} %all_refs_0_.1, bf16[256,1024]{1,0:T(8,128)(2,1)} %all_refs_1_.1, ...), custom_call_target="tpu_custom_call" | custom-call | flops 23000000512 | bytes 10000000 | tf_op jit(solution)/shard_map/pallas_call | solution.py:1134
  238.2 1.3 dynamic-slice_bitcast_fusion
  239.5 0.7 constant_dynamic-slice_fusion
  240.2 0.5 slice_bitcast_fusion
  240.7 2.7 %shard_map.255 = (bf16[256,1024]{1,0:T(8,128)(2,1)}, bf16[256,1024]{1,0:T(8,128)(2,1)}, f32[32,1024]{1,0:T(8,128)}, f32[32,1024]{1,0:T(8,128)}, f32[32,1024]{1,0...) custom-call(bf16[256,1024]{1,0:T(8,128)(2,1)} %get-tuple-element.29.out_i, ...), custom_call_target="tpu_custom_call" | custom-call | tf_op jit(solution)/shard_map/pallas_call | solution.py:1145

commit v3 on v2

--- a/solution.py
+++ b/solution.py
@@ -471,33 +471,33 @@
     local_d.wait()
     gather_pass(VECS, 0)
     gather_own(WOUT)
-    gather_pass(ATT, 0)
+    gather_pass(VECS, 1)
     spread_nbr(0, 0)
     spread_nbr(1, 0)
+    gather_pass(VECS, 2)
     pre_wait(2)
     for copy in pre_sent:
         copy.wait_send()
-    gather_pass(VECS, 1)
-    gather_pass(VECS, 2)
-    gather_own(FFN, (1, 2))
     vec_end()
     norm_one(held[0], c)
     norm_one(beside[0], c)
+    gather_pass(ATT, 0)
+    spread_own(0, 1)
+    spread_own(1, 1)
+    gather_own(FFN, (1, 2))
+    norm_one(held[1], c)
     gather_pass(ATT, 1)
     gather_pass(WOUT, 0)
     spread_own(2, 0)
-    spread_own(0, 1)
-    spread_own(1, 1)
     gather_own(FFN, (0,))
     gather_pass(ATT, 2)
-    norm_one(held[1], c)
     spread_home(2, False)
     gather_pass(WOUT, 1)
     gather_pass(WOUT, 2)
     spread_nbr(0, 1)
     spread_nbr(1, 1)
+    norm_one(beside[1], c)
     swap_out()
-    norm_one(beside[1], c)
     spread_end(0)
     spread_end(1)
     for i in held + beside:
@@ -898,13 +898,19 @@
         feed(far_tile(k))
         if k < 2:
             down_far(k)
-        up_far(k)
-    for i in range(4):
-        feed_two(i)
-        if i:
-            ex_mid(2, i - 1)
+            up_far(k)
+    feed_two(0)
+    up_far(2)
+    feed_two(1)
+    ex_mid(2, 0)
+    up_far(3)
+    feed_two(2)
+    ex_mid(2, 1)
+    feed_two(3)
+    ex_mid(2, 2)
+    feed_out(0)
     ex_mid(2, 3)
-    for i in range(4):
+    for i in (1, 2, 3):
         feed_out(i)
     feed_back(0)
     feed_back(1)
@@ -1003,41 +1009,41 @@
     feed_back(3)
     for i in range(4):
         ex_mid(1, i)
-    grad_mid(1)
     db_end(2)
+    attend_back(2)
     db_end(3)
     out_first()
-    attend_back(2)
+    grad_mid(1)
+    attend_back(3)
+
+    @pl.loop(0, 4)
+    def _(i):
+        m.QKV[row_tile(i), two : 3 * two] = m.ACC[row_tile(i), :].astype(BF16)
+
+    qkv_far()
     grad_mid(0)
     finish_out(0)
     finish_out(1)
     out_second()
-    attend_back(3)
-
-    @pl.loop(0, 4)
-    def _(i):
-        m.QKV[row_tile(i), two : 3 * two] = m.ACC[row_tile(i), :].astype(BF16)
-
-    qkv_far()
     far_close(1)
     for i in range(4):
         ex_close(1, i)
-    out_third()
     for i in range(4):
         first_back(i)
         if i:
             ex_mid(3, i - 1)
     ex_mid(3, 3)
+    out_third()
+    qkv_near()
     out_fourth()
-    qkv_near()
+    grad_mid(2)
+    grad_mid(3)
     finish_in(0)
     finish_in(1)
 
     for d in (1, 2, 3):
         tt = lax.rem(t + d, 4)
         push(m.VSUM, m.VR1.at[t], m.v1_s.at[d - 1], m.v1_r.at[t], mate(tt))
-    grad_mid(2)
-    grad_mid(3)
     rest = m.VSUM[...]
     for d in (1, 2, 3):
         tt = lax.rem(t + d, 4)

time: 247 us -> 230 us (0.931); the launches traced: 244 us -> 229 us
  Pallas kernels: 240 us -> 226 us
    pallas_call x1, Pallas kernels: 238 us -> 223 us  [call_fused(): pl.pallas_call(functools.partial(fused, names), out_shape=(tokens, tokens...]
where the time goes in v3:
time: 230 us; the launch traced here: 229 us
  Pallas kernels  226 us (98%)
  local copies, waits for them, and re-layouts  2.53 us (1%)
    pallas_call x1, Pallas kernels, call_fused(): pl.pallas_call(functools.partial(fused, names), out_shape=(tokens, tokens...  223 us

profile of v3, /device:TPU:0, one launch (start us, length us, event | category | flops | bytes accessed | tf_op | source)
XLA Modules:
  0.0 229.1 jit_solution(2786985069878886970)
XLA Ops:
  0.7 223.0 %shard_map.254 = (bf16[256,1024]{1,0:T(8,128)(2,1)}, bf16[256,1024]{1,0:T(8,128)(2,1)}, bf16[4,32,768]{2,1,0:T(8,128)(2,1)}, bf16[4,32,1024]{2,1,0:T(8,128)(2,1)...) custom-call(bf16[256,1024]{1,0:T(8,128)(2,1)} %all_refs_0_.1, bf16[256,1024]{1,0:T(8,128)(2,1)} %all_refs_1_.1, ...), custom_call_target="tpu_custom_call" | custom-call | flops 23000000512 | bytes 10000000 | tf_op jit(solution)/shard_map/pallas_call | solution.py:1140
  223.7 1.3 dynamic-slice_bitcast_fusion
  224.9 0.7 constant_dynamic-slice_fusion
  225.7 0.5 slice_bitcast_fusion
  226.2 2.7 %shard_map.255 = (bf16[256,1024]{1,0:T(8,128)(2,1)}, bf16[256,1024]{1,0:T(8,128)(2,1)}, f32[32,1024]{1,0:T(8,128)}, f32[32,1024]{1,0:T(8,128)}, f32[32,1024]{1,0...) custom-call(bf16[256,1024]{1,0:T(8,128)(2,1)} %get-tuple-element.29.out_i, ...), custom_call_target="tpu_custom_call" | custom-call | tf_op jit(solution)/shard_map/pallas_call | solution.py:1151

commit v4 on v3

--- a/solution.py
+++ b/solution.py
@@ -125,7 +125,7 @@
         VSUM=V((8, width), F32),
         VMID=V((8, width), F32),
         VR1=V((4, 8, width), F32),
-        VR2=V((8, 8, width), F32),
+        VR2=V((8, 2, 8, 128), F32),
         sp_s=dma((3, 8)),
         sp_r=dma((3, 4, 2)),
         loc=dma((4,)),
@@ -162,8 +162,8 @@
         pe_r=dma((2, 4)),
         v1_s=dma((3,)),
         v1_r=dma((4,)),
-        v2_s=dma((7,)),
-        v2_r=dma((8,)),
+        v2_s=dma((7, 2)),
+        v2_r=dma((8, 2)),
         ret_s=dma((2, 2)),
         ret_r=dma((2, 2)),
     )
@@ -485,11 +485,11 @@
     spread_own(0, 1)
     spread_own(1, 1)
     gather_own(FFN, (1, 2))
+    gather_own(FFN, (0,))
     norm_one(held[1], c)
     gather_pass(ATT, 1)
     gather_pass(WOUT, 0)
     spread_own(2, 0)
-    gather_own(FFN, (0,))
     gather_pass(ATT, 2)
     spread_home(2, False)
     gather_pass(WOUT, 1)
@@ -514,15 +514,15 @@
     def _(n):
         w = m.WA[:, :, :, :, col_tile(n)].reshape(width, 256)
 
-        @pl.loop(0, 4)
-        def _(i):
-            m.QKV[row_tile(i), col_tile(n)] = dot_nn(m.N1[row_tile(i), :], w).astype(BF16)
+        for i in range(2):
+            at = slice(2 * i * rows, (2 * i + 2) * rows)
+            m.QKV[at, col_tile(n)] = dot_nn(m.N1[at, :], w).astype(BF16)
 
     EX = (
         (m.PR0, m.RBa, m.RXa),
         (m.PR1, m.RBb, m.RXb),
         (m.PR0, m.RBa, m.RXc),
-        (m.PR1, m.RBc, m.RXd),
+        (m.PR0, m.RBc, m.RXd),
     )
     ex_open = {}
     ex_far = {1: [], 3: []}
@@ -635,9 +635,12 @@
         @pl.loop(0, width // 256)
         def _(n):
             w = m.WD[:, :, col_tile(n)].reshape(hid, 256)
-            ex_put(1, i, col_tile(n), dot_nn(m.HID[r0 : r0 + rows, :], w))
+            low = dot_nn(m.HID[r0 : r0 + 2 * rows, :], w).astype(BF16)
+            for b in range(2):
+                ex_put(1, i + b, col_tile(n), low[b * rows : (b + 1) * rows])
 
         ex_send(1, i)
+        ex_send(1, i + 1)
 
     def feed_back(i):
         xhat, rstd = norm_parts(m.RES[i])
@@ -908,10 +911,9 @@
     ex_mid(2, 1)
     feed_two(3)
     ex_mid(2, 2)
+    ex_mid(2, 3)
     feed_out(0)
-    ex_mid(2, 3)
-    for i in (1, 2, 3):
-        feed_out(i)
+    feed_out(2)
     feed_back(0)
     feed_back(1)
     down_near()
@@ -978,6 +980,7 @@
 
     def first_back(i):
         r0 = i * rows
+        ex_close(2, i)
 
         @pl.loop(0, width // 256)
         def _(n):
@@ -989,7 +992,7 @@
     def finish_in(kk):
         i = mine[kk]
         arrived(m.RXd.at[kk], m.xr.at[3, kk])
-        g = m.PR1[i, c].astype(F32) + m.RXd[kk].astype(F32)
+        g = m.PR0[i, c].astype(F32) + m.RXd[kk].astype(F32)
         xhat, rstd = norm_parts(m.X[i, c].astype(F32))
         parts = (
             jnp.sum(m.DZ[i, c].astype(F32), axis=0, keepdims=True),
@@ -1025,9 +1028,6 @@
     finish_out(0)
     finish_out(1)
     out_second()
-    far_close(1)
-    for i in range(4):
-        ex_close(1, i)
     for i in range(4):
         first_back(i)
         if i:
@@ -1044,6 +1044,11 @@
     for d in (1, 2, 3):
         tt = lax.rem(t + d, 4)
         push(m.VSUM, m.VR1.at[t], m.v1_s.at[d - 1], m.v1_r.at[t], mate(tt))
+    m.OD[...] = grad_sum(1)
+    keep_down = pltpu.make_async_copy(m.OD, m.gdn, m.loc.at[2])
+    keep_down.start()
+    m.FIU[...] = grad_sum(0).astype(BF16)
+    give(0, lambda cc, pp: m.FIU.at[pl.ds(pl.multiple_of((cc * 2 + pp) * rw, rw), rw)], m.peu)
     rest = m.VSUM[...]
     for d in (1, 2, 3):
         tt = lax.rem(t + d, 4)
@@ -1051,14 +1056,17 @@
         rest = rest + m.VR1[tt]
     row8 = lax.broadcasted_iota(jnp.int32, (8, width), 0)
     m.VMID[...] = jnp.where(row8 == 5, m.VSUM[...], rest)
+    def vec_parts(yy, xx, qq):
+        return [
+            m.VMID.at[:, pl.ds(pl.multiple_of(at * 128, 128), 128)]
+            for at in ((yy * 2 + xx) * 2 + c, at8(yy, xx, qq))
+        ]
+
     for k, f in enumerate(flips):
         if k:
-            push(m.VMID, m.VR2.at[me], m.v2_s.at[k - 1], m.v2_r.at[me], peer(*flipped(*f)))
-    m.OD[...] = grad_sum(1)
-    keep_down = pltpu.make_async_copy(m.OD, m.gdn, m.loc.at[2])
-    keep_down.start()
-    m.FIU[...] = grad_sum(0).astype(BF16)
-    give(0, lambda cc, pp: m.FIU.at[pl.ds(pl.multiple_of((cc * 2 + pp) * rw, rw), rw)], m.peu)
+            spot = flipped(*f)
+            for e, part in enumerate(vec_parts(*spot)):
+                push(part, m.VR2.at[me, e], m.v2_s.at[k - 1, e], m.v2_r.at[me, e], peer(*spot))
     out_sum()
     keep_out = pltpu.make_async_copy(m.OO, m.go, m.loc.at[3])
     keep_out.start()
@@ -1066,13 +1074,14 @@
         m.FIN[e] = grad_sum(2 + e).astype(BF16)
     give(1, lambda cc, pp: m.FIN.at[cc, pl.ds(pl.multiple_of(pp * rw, rw), rw)], m.peq)
 
-    final = m.VMID[...]
-    for k, f in enumerate(flips):
-        if k:
-            at = at8(*flipped(*f))
-            arrived(m.VR2.at[at], m.v2_r.at[at])
-            final = final + m.VR2[at]
-    m.gvec[...] = final
+    for e, part in enumerate(vec_parts(y, x, q)):
+        final = part[...]
+        for k, f in enumerate(flips):
+            if k:
+                at = at8(*flipped(*f))
+                arrived(m.VR2.at[at, e], m.v2_r.at[at, e])
+                final = final + m.VR2[at, e]
+        m.gvec[e] = final
 
     for k, dst in enumerate((m.out, m.ig)):
         for cc in range(2):
@@ -1084,6 +1093,7 @@
         copy.wait_send()
     for e, i in ex_open:
         ex_close(e, i)
+    far_close(1)
     far_close(3)
     for near, copy in homes:
 
@@ -1126,10 +1136,7 @@
     hid = w_up.shape[1] // RANKS
     rw, fw = w_query.shape[0], w_down.shape[0]
     shapes = scratch_of(rows, width, hid, rw, fw)
-    dp, blk = lax.axis_index("dp"), lax.axis_index("blk")
-    n_blk = lax.axis_size("blk")
-    place = dp * n_blk + blk
-    at_up = dp // 2 * 2 + blk // 2
+    blk = lax.axis_index("blk")
     small_in = [v.reshape(1, -1) for v in (down_bias, ln1_gain, ln1_bias, ln2_gain, ln2_bias, up_bias)]
     names = IN_NAMES + OUT_NAMES + tuple(shapes)
     any_, vm = pl.BlockSpec(memory_space=pl.ANY), pl.BlockSpec(memory_space=pltpu.VMEM)
@@ -1139,7 +1146,7 @@
     moved = (S((RANKS, rw, cols), BF16), S((RANKS, rw, hid), BF16))
     out, ig, peq, peu, go, gdn, gvec = pl.pallas_call(
         functools.partial(fused, names),
-        out_shape=(tokens, tokens) + moved + (wide, S(w_down.shape, F32), S((8, width), F32)),
+        out_shape=(tokens, tokens) + moved + (wide, S(w_down.shape, F32), S((2, 8, 128), F32)),
         in_specs=[any_, any_, vm] + [any_] * 6 + [vm] * 6,
         out_specs=[any_] * 6 + [vm],
         scratch_shapes=list(shapes.values()),
@@ -1166,8 +1173,8 @@
         ],
         compiler_params=pltpu.CompilerParams(vmem_limit_bytes=VMEM_BYTES),
     )(out, ig, peq, peu, go, gdn)
-    small = lax.dynamic_slice(gvec, (0, place * rw), (5, rw))
-    gup_bias = lax.dynamic_slice(gvec, (5, at_up * fw), (1, fw))[0]
+    small = lax.dynamic_slice(gvec[0], (0, blk * rw), (5, rw))
+    gup_bias = gvec[1, 5]
     return (out, ig, gq, gk, gv, go, gup, gdn, gup_bias, small[0], small[1], small[2], small[3], small[4])
 
 

time: 230 us -> 225 us (0.978)
  Pallas kernels: 226 us -> 221 us
    pallas_call x1, Pallas kernels: 223 us -> 219 us  [call_fused(): pl.pallas_call(functools.partial(fused, names), out_shape=(tokens, tokens...]
where the time goes in v4:
time: 225 us; the launch traced here: 224 us
  Pallas kernels  221 us (98%)
    pallas_call x1, Pallas kernels, call_fused(): pl.pallas_call(functools.partial(fused, names), out_shape=(tokens, tokens...  219 us

profile of v4, /device:TPU:0, one launch (start us, length us, event | category | flops | bytes accessed | tf_op | source)
XLA Modules:
  0.0 224.2 jit_solution(16803426706142110219)
XLA Ops:
  0.7 218.8 %shard_map.254 = (bf16[256,1024]{1,0:T(8,128)(2,1)}, bf16[256,1024]{1,0:T(8,128)(2,1)}, bf16[4,32,768]{2,1,0:T(8,128)(2,1)}, bf16[4,32,1024]{2,1,0:T(8,128)(2,1)...) custom-call(bf16[256,1024]{1,0:T(8,128)(2,1)} %all_refs_0_.1, bf16[256,1024]{1,0:T(8,128)(2,1)} %all_refs_1_.1, ...), custom_call_target="tpu_custom_call" | custom-call | flops 23000000512 | bytes 10000000 | tf_op jit(solution)/shard_map/pallas_call | solution.py:1147
  219.5 0.0 copy-start
  219.5 0.7 copy-done
  220.2 0.5 slice_bitcast_fusion.5
  220.7 0.1 constant_dynamic-slice_fusion
  220.7 0.5 slice_bitcast_fusion
  221.3 2.7 %shard_map.255 = (bf16[256,1024]{1,0:T(8,128)(2,1)}, bf16[256,1024]{1,0:T(8,128)(2,1)}, f32[32,1024]{1,0:T(8,128)}, f32[32,1024]{1,0:T(8,128)}, f32[32,1024]{1,0...) custom-call(bf16[256,1024]{1,0:T(8,128)(2,1)} %get-tuple-element.29.out_i, ...), custom_call_target="tpu_custom_call" | custom-call | tf_op jit(solution)/shard_map/pallas_call | solution.py:1158
  (1 shorter events, 0.0 us)
Async XLA Ops:
  219.5 0.7 copy-start

commit v5 on v4

--- a/solution.py
+++ b/solution.py
@@ -981,13 +981,16 @@
     def first_back(i):
         r0 = i * rows
         ex_close(2, i)
+        ex_close(2, i + 1)
 
         @pl.loop(0, width // 256)
         def _(n):
-            w = m.WA[n].reshape(256, cols)
-            ex_put(3, i, col_tile(n), dot_nt(m.QKV[r0 : r0 + rows, :], w))
+            low = dot_nt(m.QKV[r0 : r0 + 2 * rows, :], m.WA[n].reshape(256, cols)).astype(BF16)
+            for b in range(2):
+                ex_put(3, i + b, col_tile(n), low[b * rows : (b + 1) * rows])
 
         ex_send(3, i)
+        ex_send(3, i + 1)
 
     def finish_in(kk):
         i = mine[kk]
@@ -1028,11 +1031,10 @@
     finish_out(0)
     finish_out(1)
     out_second()
+    first_back(0)
+    first_back(2)
     for i in range(4):
-        first_back(i)
-        if i:
-            ex_mid(3, i - 1)
-    ex_mid(3, 3)
+        ex_mid(3, i)
     out_third()
     qkv_near()
     out_fourth()
@@ -1044,11 +1046,11 @@
     for d in (1, 2, 3):
         tt = lax.rem(t + d, 4)
         push(m.VSUM, m.VR1.at[t], m.v1_s.at[d - 1], m.v1_r.at[t], mate(tt))
+    m.FIU[...] = grad_sum(0).astype(BF16)
+    give(0, lambda cc, pp: m.FIU.at[pl.ds(pl.multiple_of((cc * 2 + pp) * rw, rw), rw)], m.peu)
     m.OD[...] = grad_sum(1)
     keep_down = pltpu.make_async_copy(m.OD, m.gdn, m.loc.at[2])
     keep_down.start()
-    m.FIU[...] = grad_sum(0).astype(BF16)
-    give(0, lambda cc, pp: m.FIU.at[pl.ds(pl.multiple_of((cc * 2 + pp) * rw, rw), rw)], m.peu)
     rest = m.VSUM[...]
     for d in (1, 2, 3):
         tt = lax.rem(t + d, 4)

time: 225 us -> 225 us (level)
  no operation moved by 1% of the time
where the time goes in v5:
time: 225 us; the launch traced here: 224 us
  Pallas kernels  222 us (99%)
    pallas_call x1, Pallas kernels, call_fused(): pl.pallas_call(functools.partial(fused, names), out_shape=(tokens, tokens...  219 us

profile of v5, /device:TPU:0, one launch (start us, length us, event | category | flops | bytes accessed | tf_op | source)
XLA Modules:
  0.0 224.3 jit_solution(15429503913672506694)
XLA Ops:
  0.7 218.9 %shard_map.254 = (bf16[256,1024]{1,0:T(8,128)(2,1)}, bf16[256,1024]{1,0:T(8,128)(2,1)}, bf16[4,32,768]{2,1,0:T(8,128)(2,1)}, bf16[4,32,1024]{2,1,0:T(8,128)(2,1)...) custom-call(bf16[256,1024]{1,0:T(8,128)(2,1)} %all_refs_0_.1, bf16[256,1024]{1,0:T(8,128)(2,1)} %all_refs_1_.1, ...), custom_call_target="tpu_custom_call" | custom-call | flops 23000000512 | bytes 10000000 | tf_op jit(solution)/shard_map/pallas_call | solution.py:1149
  219.6 0.0 copy-start
  219.6 0.7 copy-done
  220.3 0.5 slice_bitcast_fusion.5
  220.8 0.1 constant_dynamic-slice_fusion
  220.9 0.5 slice_bitcast_fusion
  221.4 2.7 %shard_map.255 = (bf16[256,1024]{1,0:T(8,128)(2,1)}, bf16[256,1024]{1,0:T(8,128)(2,1)}, f32[32,1024]{1,0:T(8,128)}, f32[32,1024]{1,0:T(8,128)}, f32[32,1024]{1,0...) custom-call(bf16[256,1024]{1,0:T(8,128)(2,1)} %get-tuple-element.29.out_i, ...), custom_call_target="tpu_custom_call" | custom-call | tf_op jit(solution)/shard_map/pallas_call | solution.py:1160
  (1 shorter events, 0.0 us)
Async XLA Ops:
  219.6 0.7 copy-start
